TPU v7x, 32 devices: a whole 2x2x4 slice. The times are simulated.
32 devices in a mesh: dp: 2 (over x), blk: 4 (over z), mp: 4 (over y, core).
Axes of the slice: x: 2, y: 2, z: 4, core: 2. Of those that a mesh axis runs over, the one named last changes fastest.
Arguments:
- inputs: bfloat16 [8, 512, 2048], P('dp', 'blk'), may hold values from -6 to 6
- lengths: int32 [8], P('dp'), may hold values from 288 to 512, as said below
- w_qkv: bfloat16 [2048, 3, 2048], P(None, None, 'mp'), may hold values from -0.125 to 0.125
- b_qv: bfloat16 [2, 2048], P(None, 'mp'), may hold values from -3 to 3
- w_out: bfloat16 [2048, 2048], P(None, 'mp'), may hold values from -0.5 to 0.5
- out_biases: bfloat16 [2, 2048], replicated, may hold values from -2 to 2
- ln_gains: bfloat16 [2, 2048], replicated, may hold values from 0.25 to 1.75
- ln_shifts: bfloat16 [2, 2048], replicated, may hold values from -2 to 2
- w_up: bfloat16 [2048, 8192], P(None, 'mp'), may hold values from -0.125 to 0.125
- b_up: bfloat16 [8192], P('mp'), may hold values from -3 to 3
- w_down: bfloat16 [2048, 8192], P(None, 'mp'), may hold values from -0.0625 to 0.0625
- cotangent: bfloat16 [8, 512, 2048], P('dp', 'blk'), may hold values from -6 to 6
Outputs:
- output: bfloat16 [8, 512, 2048], P('dp', 'blk')
- input_grad: float32 [8, 512, 2048], P('dp', 'blk')
- grad_qkv: float32 [2048, 3, 2048], P(('dp', 'blk'), None, 'mp')
- grad_qv_bias: float32 [2, 2048], P(None, 'mp')
- grad_out: float32 [2048, 2048], P(('dp', 'blk'), 'mp')
- grad_out_biases: float32 [2, 2048], replicated
- grad_gains: float32 [2, 2048], replicated
- grad_shifts: float32 [2, 2048], replicated
- grad_up: float32 [2048, 8192], P(('dp', 'blk'), 'mp')
- grad_up_bias: float32 [8192], P('mp')
- grad_down: float32 [2048, 8192], P(('dp', 'blk'), 'mp')
Inputs may be any that keep to these rules, and one draw needn't show every extreme that they name: `lengths`: each length is 256 plus a positive multiple of 32; in each aligned block of 4 items one item, drawn from the seed, has length 512.
All inputs are finite; a program needn't handle non-finite values.
Results may differ from a plain program's by a relative error of at most 0.019.
Values may be sent and summed in bfloat16 or wider, within the bound.
No kernel may reach another device: no remote copies, remote signals or barrier semaphores. Data moves between devices by JAX's collectives and lax.ppermute only.
A program may use at most 192 MiB of HBM per device.

v0:
```python
import jax
import jax.numpy as jnp
from jax import lax
from jax.sharding import PartitionSpec as P

DH = 128


def layer_norm(values, gain, shift):
    centered = values - jnp.mean(values, axis=-1, keepdims=True)
    variance = jnp.mean(centered * centered, axis=-1, keepdims=True)
    inverse = lax.rsqrt(variance + 1e-05)
    unit = centered * inverse
    return (unit * gain + shift, unit, inverse)


def norm_back(grad_norm, unit, inverse, gain):
    scaled = grad_norm * gain
    first = jnp.mean(scaled, axis=-1, keepdims=True)
    second = jnp.mean(scaled * unit, axis=-1, keepdims=True)
    return inverse * (scaled - first - unit * second)


def exact_gelu(values):
    return jax.nn.gelu(values, approximate=False)


def contract_rows(left, right):
    return lax.dot_general(
        left, right, (((0,), (0,)), ((), ())), preferred_element_type=jnp.float32
    )


def contract_cols(left, right):
    return lax.dot_general(
        left, right, (((1,), (1,)), ((), ())), preferred_element_type=jnp.float32
    )


def on_device(
    inputs,
    lengths,
    w_qkv,
    b_qv,
    w_out,
    out_biases,
    ln_gains,
    ln_shifts,
    w_up,
    b_up,
    w_down,
    cotangent,
):
    items, block_len, d_model = inputs.shape
    rows = items * block_len
    width = w_qkv.shape[2]
    local_heads = width // DH
    scale = DH ** (-0.5)
    gains = ln_gains.astype(jnp.float32)
    shifts = ln_shifts.astype(jnp.float32)
    biases = out_biases.astype(jnp.float32)
    positions = lax.axis_index("blk") * block_len + jnp.arange(block_len, dtype=jnp.int32)
    valid = positions[None, :] < lengths[:, None]
    flat = inputs.reshape(rows, d_model).astype(jnp.float32)
    normed_one, unit_one, inverse_one = layer_norm(flat, gains[0], shifts[0])
    act_one = normed_one.astype(jnp.bfloat16)
    projected = jnp.einsum("rd,dth->trh", act_one, w_qkv, preferred_element_type=jnp.float32)
    qv_bias = b_qv.astype(jnp.float32)
    queries = (
        (projected[0] + qv_bias[0]).astype(jnp.bfloat16).reshape(items, block_len, local_heads, DH)
    )
    keys_local = projected[1].astype(jnp.bfloat16).reshape(items, block_len, width)
    values_local = (projected[2] + qv_bias[1]).astype(jnp.bfloat16).reshape(items, block_len, width)
    keys_whole, values_whole = (
        lax.all_gather(keys_local, "blk", axis=1, tiled=True),
        lax.all_gather(values_local, "blk", axis=1, tiled=True),
    )
    full_len = keys_whole.shape[1]
    key_pos = jnp.arange(full_len, dtype=jnp.int32)
    allowed = (key_pos[None, None, None, :] <= positions[None, None, :, None]) & (
        key_pos[None, None, None, :] < lengths[:, None, None, None]
    )

    def make_scores(query_heads, key_rows):
        key_heads = key_rows.reshape(items, full_len, local_heads, DH)
        raw = jnp.einsum(
            "icnd,ijnd->incj", query_heads, key_heads, preferred_element_type=jnp.float32
        )
        return jnp.where(allowed, raw * scale, -1e30)

    scores = make_scores(queries, keys_whole)
    peak = jnp.max(scores, axis=-1, keepdims=True)
    expo = jnp.exp(scores - peak)
    total = jnp.sum(expo, axis=-1, keepdims=True)
    probs = expo / total
    log_total = peak + jnp.log(total)
    value_heads = values_whole.reshape(items, full_len, local_heads, DH)
    mixed = jnp.einsum(
        "incj,ijnd->icnd",
        probs.astype(jnp.bfloat16),
        value_heads,
        preferred_element_type=jnp.float32,
    )
    mixed = mixed.reshape(rows, width).astype(jnp.bfloat16)
    attn = lax.psum(contract_cols(mixed, w_out), "mp") + biases[0]
    resid = flat + attn
    normed_two, unit_two, inverse_two = layer_norm(resid, gains[1], shifts[1])
    act_two = normed_two.astype(jnp.bfloat16)
    upper = jnp.dot(act_two, w_up, preferred_element_type=jnp.float32) + b_up.astype(jnp.float32)
    gelu_vals, gelu_back = jax.vjp(exact_gelu, upper)
    gelu_low = gelu_vals.astype(jnp.bfloat16)
    down = (
        lax.psum(contract_cols(gelu_low, w_down).astype(jnp.bfloat16), "mp").astype(jnp.float32)
        + biases[1]
    )
    output = (resid + down).astype(jnp.bfloat16).reshape(items, block_len, d_model)
    grad_y = cotangent.reshape(rows, d_model).astype(jnp.float32) * valid.reshape(rows, 1).astype(
        jnp.float32
    )
    grad_y_low = grad_y.astype(jnp.bfloat16)
    grad_down_local = contract_rows(grad_y_low, gelu_low)
    grad_gelu = jnp.dot(grad_y_low, w_down, preferred_element_type=jnp.float32)
    grad_upper = gelu_back(grad_gelu)[0].astype(jnp.bfloat16)
    grad_up_local = contract_rows(act_two, grad_upper)
    grad_up_bias = jnp.sum(grad_upper.astype(jnp.float32), axis=0)
    grad_act_two = lax.psum(contract_cols(grad_upper, w_up).astype(jnp.bfloat16), "mp").astype(
        jnp.float32
    )
    grad_resid = grad_y + norm_back(grad_act_two, unit_two, inverse_two, gains[1])
    gain_two = jnp.sum(grad_act_two * unit_two, axis=0)
    shift_two = jnp.sum(grad_act_two, axis=0)
    grad_attn = grad_resid.astype(jnp.bfloat16)
    attn_bias_grad = jnp.sum(grad_attn.astype(jnp.float32), axis=0)
    down_bias_grad = jnp.sum(grad_y, axis=0)
    grad_out_local = contract_rows(grad_attn, mixed)
    grad_mixed = jnp.dot(grad_attn, w_out, preferred_element_type=jnp.float32).astype(jnp.bfloat16)
    grad_mixed = grad_mixed.reshape(items, block_len, local_heads, DH)
    keys_back, values_back = (keys_whole, values_whole)
    key_heads = keys_back.reshape(items, full_len, local_heads, DH)
    value_back_heads = values_back.reshape(items, full_len, local_heads, DH)
    probs_again = jnp.exp(make_scores(queries, keys_back) - log_total)
    grad_values = jnp.einsum(
        "incj,icnd->ijnd",
        probs_again.astype(jnp.bfloat16),
        grad_mixed,
        preferred_element_type=jnp.float32,
    )
    grad_probs = jnp.einsum(
        "icnd,ijnd->incj", grad_mixed, value_back_heads, preferred_element_type=jnp.float32
    )
    row_terms = jnp.sum(probs_again * grad_probs, axis=-1, keepdims=True)
    grad_scores = (probs_again * (grad_probs - row_terms) * scale).astype(jnp.bfloat16)
    grad_queries = jnp.einsum(
        "incj,ijnd->icnd", grad_scores, key_heads, preferred_element_type=jnp.float32
    )
    grad_queries = grad_queries.astype(jnp.bfloat16).reshape(rows, width)
    grad_keys = jnp.einsum(
        "incj,icnd->ijnd", grad_scores, queries, preferred_element_type=jnp.float32
    )
    grad_keys_own, grad_values_own = (
        lax.psum_scatter(
            grad_keys.reshape(items, full_len, width), "blk", scatter_dimension=1, tiled=True
        ),
        lax.psum_scatter(
            grad_values.reshape(items, full_len, width), "blk", scatter_dimension=1, tiled=True
        ),
    )
    grad_keys_low = grad_keys_own.astype(jnp.bfloat16).reshape(rows, width)
    grad_values_low = grad_values_own.astype(jnp.bfloat16).reshape(rows, width)
    qv_bias_grad = jnp.stack(
        [
            jnp.sum(grad_queries.astype(jnp.float32), axis=0),
            jnp.sum(grad_values_low.astype(jnp.float32), axis=0),
        ]
    )
    grad_stack = jnp.stack([grad_queries, grad_keys_low, grad_values_low])
    grad_qkv_local = jnp.einsum(
        "rd,trh->dth", act_one, grad_stack, preferred_element_type=jnp.float32
    )
    grad_act_one = lax.psum(
        jnp.einsum("trh,dth->rd", grad_stack, w_qkv, preferred_element_type=jnp.float32).astype(
            jnp.bfloat16
        ),
        "mp",
    ).astype(jnp.float32)
    input_grad = grad_resid + norm_back(grad_act_one, unit_one, inverse_one, gains[0])
    gain_one = jnp.sum(grad_act_one * unit_one, axis=0)
    shift_one = jnp.sum(grad_act_one, axis=0)
    grad_qkv_part, grad_out_part, grad_up_part, grad_down_part = (
        lax.psum_scatter(
            grad_qkv_local.astype(jnp.bfloat16), ("dp", "blk"), scatter_dimension=0, tiled=True
        ).astype(jnp.float32),
        lax.psum_scatter(
            grad_out_local.astype(jnp.bfloat16), ("dp", "blk"), scatter_dimension=0, tiled=True
        ).astype(jnp.float32),
        lax.psum_scatter(
            grad_up_local.astype(jnp.bfloat16), ("dp", "blk"), scatter_dimension=0, tiled=True
        ).astype(jnp.float32),
        lax.psum_scatter(
            grad_down_local.astype(jnp.bfloat16), ("dp", "blk"), scatter_dimension=0, tiled=True
        ).astype(jnp.float32),
    )
    grad_gains, grad_shifts, grad_out_biases, grad_qv_bias, grad_up_sum = (
        lax.psum(jnp.stack([gain_one, gain_two]).astype(jnp.bfloat16), ("dp", "blk")).astype(
            jnp.float32
        ),
        lax.psum(jnp.stack([shift_one, shift_two]).astype(jnp.bfloat16), ("dp", "blk")).astype(
            jnp.float32
        ),
        lax.psum(
            jnp.stack([attn_bias_grad, down_bias_grad]).astype(jnp.bfloat16), ("dp", "blk")
        ).astype(jnp.float32),
        lax.psum(qv_bias_grad.astype(jnp.bfloat16), ("dp", "blk")).astype(jnp.float32),
        lax.psum(grad_up_bias.astype(jnp.bfloat16), ("dp", "blk")).astype(jnp.float32),
    )
    return (
        output,
        input_grad.reshape(items, block_len, d_model),
        grad_qkv_part,
        grad_qv_bias,
        grad_out_part,
        grad_out_biases,
        grad_gains,
        grad_shifts,
        grad_up_part,
        grad_up_sum,
        grad_down_part,
    )


def solution(mesh):
    in_specs = (
        P("dp", "blk", None),
        P("dp"),
        P(None, None, "mp"),
        P(None, "mp"),
        P(None, "mp"),
        P(),
        P(),
        P(),
        P(None, "mp"),
        P("mp"),
        P(None, "mp"),
        P("dp", "blk", None),
    )
    out_specs = (
        P("dp", "blk", None),
        P("dp", "blk", None),
        P(("dp", "blk"), None, "mp"),
        P(None, "mp"),
        P(("dp", "blk"), "mp"),
        P(),
        P(),
        P(),
        P(("dp", "blk"), "mp"),
        P("mp"),
        P(("dp", "blk"), "mp"),
    )
    return jax.shard_map(
        on_device, mesh=mesh, in_specs=in_specs, out_specs=out_specs, check_vma=False
    )
```

profile of v0, /device:TPU:0, one launch (start us, length us, event | category | flops | bytes accessed | tf_op | source)
XLA Modules:
  0.0 1085.7 jit_solution(5554954755769135744)
XLA Ops:
  7.3 2.1 convert_reduce_fusion
  9.4 3.0 fusion.19
  14.0 3.4 fusion.55
  17.4 1.7 copy-done.15
  19.1 1.0 copy.34
  20.2 1.7 fusion.87
  22.0 0.9 add_convert_fusion.4
  23.0 1.3 squeeze.8
  24.3 1.6 copy.33
  26.2 43.1 %all-gather.5.cloned.1.call-done = bf16[4,512,512]{1,2,0:T(8,128)(2,1)} async-done(((bf16[4,128,512]{1,2,0:T(8,128)(2,1)}), bf16[4,512,512]{1,2,0:T(8,128)(2,1)}) %all-gather.5.cloned.1.call-update) | async-done | bytes 2097168 | tf_op jit(solution)/shard_map/all_gather | solution.py:75
  69.3 2.7 fusion.92
  72.0 2.0 copy-done.9
  74.0 1.2 fusion.32
  75.2 40.4 %all-gather.3.cloned.1.call-done = bf16[4,512,512]{2,1,0:T(8,128)(2,1)} async-done(((bf16[4,128,512]{2,1,0:T(8,128)(2,1)}), bf16[4,512,512]{2,1,0:T(8,128)(2,1)}) %all-gather.3.cloned.1.call-update) | async-done | bytes 2097168 | tf_op jit(solution)/shard_map/all_gather | solution.py:76
  115.6 4.1 copy.32
  119.7 4.1 fusion.62
  124.1 3.3 fusion.67
  128.2 3.3 fusion.31
  131.5 80.3 %all-reduce.6.cloned.1.call-done = f32[512,2048]{1,0:T(8,128)} async-done(((f32[512,2048]{1,0:T(8,128)}), f32[512,2048]{1,0:T(8,128)}) %all-reduce.6.cloned.1.call-update) | async-done | bytes 4194320 | tf_op jit(solution)/shard_map/psum | solution.py:105
  211.8 3.5 fusion.86
  215.9 1.5 copy-done.2
  217.5 7.8 fusion.81
  225.3 15.5 %fusion.82 = (bf16[2048]{0:T(1024)(128)(2,1)S(1)}, bf16[512,2048]{1,0:T(8,128)(2,1)S(1)}, f32[512,2048]{1,0:T(8,128)}) fusion(f32[512,2048]{1,0:T(8,128)S(1)} %fusion.81, f32[2048]{0:T(1024)S(1)} %convert_element_type.205, bf16[512,2048]{1,0:T(8,128)(2,1)S(1)} %copy-done.19, bf16[2048,2048]{1,0:T(8,128)(2,1)S(1)} %bitcast.147), kind=kOutput, calls=%fused_computation.130 | convolution fusion | flops 4372559872 | bytes 20983808 | tf_op jit(solution)/shard_map/dot_general | solution.py:122
  240.8 1.4 copy-done.36
  242.2 5.8 convolution_convert_fusion.4
  248.2 51.4 %all-reduce.8.cloned.1.call-done = bf16[512,2048]{1,0:T(8,128)(2,1)} async-done(((bf16[512,2048]{1,0:T(8,128)(2,1)}), bf16[512,2048]{1,0:T(8,128)(2,1)}) %all-reduce.8.cloned.1.call-update) | async-done | bytes 2097168 | tf_op jit(solution)/shard_map/psum | solution.py:126
  299.7 4.7 fusion.11
  304.4 4.5 convert_reduce_fusion.1
  309.0 2.1 copy-done.7
  311.1 1.3 convolution_convert_fusion.6
  312.8 4.4 fusion.96
  317.2 16.3 %fusion.37 = f32[4,4,128,512]{3,2,1,0:T(8,128)} fusion(f32[4,4,128,512]{3,2,1,0:T(8,128)} %fusion.96, f32[4,4,128,512]{3,2,1,0:T(8,128)} %copy-done.9, f32[4,4,128]{2,1,0:T(4,128)S(1)} %bitcast.130, f32[4,128,4,128]{1,3,2,0:T(8,128)S(1)} %copy-done.13, f32[4,128]{1,0:T(4,128)S(1)} %bitcast.138), kind=kOutput, calls=%fused_computation.72 | convolution fusion | flops 276302336 | bytes 13641728 | tf_op jit(solution)/shard_map/incj,icnd->ijnd/dot_general | solution.py:157
  333.6 5.0 fusion.42
  338.6 5.6 convolution_convert_fusion.3
  344.5 4.5 multiply_convert_fusion.1
  349.0 1.3 copy-done.21
  350.3 9.2 convolution_convert_fusion.5
  359.5 14.8 %fusion.93 = (bf16[4,128]{1,0:T(4,128)(2,1)S(1)}, bf16[4,128,4,128]{3,1,2,0:T(8,128)(2,1)S(1)}) fusion(bf16[4,512,4,128]{1,3,2,0:T(8,128)(2,1)S(1)} %bitcast.115, f32[4,4,128,512]{3,2,1,0:T(8,128)} %fusion.96, f32[4,4,128,512]{3,2,1,0:T(8,128)} %copy-done.9, f32[4,4,128]{2,1,0:T(4,128)S(1)} %bitcast.132), kind=kOutput, calls=%fused_computation.139 | convolution fusion | flops 276301824 | bytes 11019264 | tf_op jit(solution)/shard_map/incj,ijnd->icnd/dot_general | solution.py:153
  375.0 35.5 %reduce-scatter.7.cloned.1.call-done = f32[4,128,512]{1,2,0:T(8,128)} async-done(((f32[4,512,512]{1,2,0:T(8,128)}), f32[4,128,512]{1,2,0:T(8,128)}) %reduce-scatter.7.cloned.1.call-update) | async-done | bytes 1048592 | tf_op jit(solution)/shard_map/reduce_scatter | solution.py:161
  410.5 1.3 convert_element_type.223
  412.0 78.0 %reduce-scatter.9.cloned.1.call-done = f32[4,128,512]{1,2,0:T(8,128)} async-done(((f32[4,512,512]{1,2,0:T(8,128)}), f32[4,128,512]{1,2,0:T(8,128)}) %reduce-scatter.9.cloned.1.call-update) | async-done | bytes 1048592 | tf_op jit(solution)/shard_map/reduce_scatter | solution.py:164
  490.0 1.4 fusion.85
  491.7 7.6 bitcast_convert_fusion
  499.3 1.5 copy-done.37
  500.9 9.5 convolution_convert_fusion.1
  510.7 1.3 copy-done.20
  512.0 8.3 convolution_convert_fusion
  520.4 1.5 copy-done.18
  521.9 6.4 convolution_convert_fusion.2
  528.4 2.2 multiply_reduce_fusion
  530.7 31.0 %reduce-scatter.13.cloned.1.call-done = bf16[256,512]{1,0:T(8,128)(2,1)} async-done(((bf16[2048,512]{1,0:T(8,128)(2,1)}), bf16[256,512]{1,0:T(8,128)(2,1)}) %reduce-scatter.13.cloned.1.call-update) | async-done | bytes 262160 | tf_op jit(solution)/shard_map/reduce_scatter | solution.py:193
  561.7 1.8 convert_element_type.234
  563.5 86.5 %all-reduce.10.cloned.1.call-done = (bf16[512,2048]{1,0:T(8,128)(2,1)}, bf16[512,2048]{1,0:T(8,128)(2,1)}) async-done(((bf16[512,2048]{1,0:T(8,128)(2,1)}, bf16[512,2048]{1,0:T(8,128)(2,1)}), (bf16[512,2048]{1,0:T(8,128)(2,1)}, bf16[512,2048]{1,0:T(8,128)(2,1)})) %all-reduce.10.cloned.1.call-update) | async-done | bytes 4194320 | tf_op jit(solution)/shard_map/psum | solution.py:113
  650.0 2.0 reduce.9
  652.0 3.5 fusion.16
  655.5 39.5 %all-reduce = (bf16[2,512]{1,0:T(2,128)(2,1)S(1)}, bf16[2,2048]{1,0:T(2,128)(2,1)S(1)}, bf16[2,2048]{1,0:T(2,128)(2,1)S(1)}, bf16[2,2048]{1,0:T(2,128)(2,1)S(1)}, bf16[2048]{0:T(1024)(128)(2,1)S(1)}) all-reduce(bf16[2,512]{1,0:T(2,128)(2,1)S(1)} %pad_maximum_fusion.6, ...), channel_id=1, replica_groups=mesh['dp'=2,'blk'=4,'mp'=4] {'dp','blk'}, use_global_device_ids=true, to_apply=%region_20.21 | all-reduce | flops 15360 | bytes 61440 | tf_op jit(solution)/shard_map/psum | solution.py:213
  698.0 5.1 add_convert_fusion.1
  704.4 3.1 fusion.14
  707.4 95.8 %reduce-scatter.15.cloned.1.call-done = bf16[256,2048]{1,0:T(8,128)(2,1)} async-done(((bf16[2048,2048]{1,0:T(8,128)(2,1)}), bf16[256,2048]{1,0:T(8,128)(2,1)}) %reduce-scatter.15.cloned.1.call-update) | async-done | bytes 1048592 | tf_op jit(solution)/shard_map/reduce_scatter | solution.py:196
  803.3 2.8 convert_element_type.242
  806.1 148.8 %reduce-scatter.17.cloned.1.call-done = bf16[256,2048]{1,0:T(8,128)(2,1)} async-done(((bf16[2048,2048]{1,0:T(8,128)(2,1)}), bf16[256,2048]{1,0:T(8,128)(2,1)}) %reduce-scatter.17.cloned.1.call-update) | async-done | bytes 1048592 | tf_op jit(solution)/shard_map/reduce_scatter | solution.py:199
  954.8 2.8 convert_element_type.245
  957.6 118.6 %reduce-scatter.11.cloned.1.call-done = bf16[256,3,512]{2,0,1:T(8,128)(2,1)} async-done(((bf16[2048,3,512]{2,0,1:T(8,128)(2,1)}), bf16[256,3,512]{2,0,1:T(8,128)(2,1)}) %reduce-scatter.11.cloned.1.call-update) | async-done | bytes 786448 | tf_op jit(solution)/shard_map/reduce_scatter | solution.py:190
  1076.3 2.5 convert_element_type.229
  (144 shorter events, 10.7 us)
Async XLA Ops:
  7.2 117.0 %copy-start = (bf16[2048,512]{1,0:T(8,128)(2,1)S(1)}, bf16[2048,512]{1,0:T(8,128)(2,1)}, u32[]{:S(2)}) copy-start(bf16[2048,512]{1,0:T(8,128)(2,1)} %param.16) | copy-start | bytes 6291460
  7.2 5.2 copy-start.29
  7.2 5.3 copy-start.30
  7.2 62.0 %all-gather.5.cloned.1.call-start = ((), (), s32[]{:S(2)}) async-start(), calls=%async_computation.7 | async-start | bytes 2621440 | tf_op jit(solution)/shard_map/all_gather | solution.py:75
  7.3 5.8 copy-start.4
  7.3 6.7 copy-start.35
  9.4 3.1 copy-start.25
  12.4 0.6 copy-start.27
  12.5 0.6 copy-start.23
  13.9 3.4 copy-start.17
  14.0 6.3 copy-start.32
  17.4 1.7 copy-start.15
  20.2 95.4 %all-gather.3.cloned.1.call-start = ((), (), s32[]{:S(2)}) async-start(), calls=%async_computation.6 | async-start | bytes 2621440 | tf_op jit(solution)/shard_map/all_gather | solution.py:76
  22.0 3.9 copy-start.34
  22.9 188.9 %all-reduce.6.cloned.1.call-start = ((), (), s32[]{:S(2)}) async-start(), calls=%async_computation.8 | async-start | bytes 8388608 | tf_op jit(solution)/shard_map/psum | solution.py:105
  25.8 49.4 %copy-start.12 = (f32[4,128,4,128]{1,3,2,0:T(8,128)}, f32[4,128,4,128]{1,3,2,0:T(8,128)S(1)}, u32[]{:S(2)}) copy-start(f32[4,128,4,128]{1,3,2,0:T(8,128)S(1)} %copy.33) | copy-start | bytes 3145732
  72.0 2.0 copy-start.9
  127.4 0.7 copy-start.33
  127.4 0.8 copy-start.31
  127.4 172.2 %all-reduce.8.cloned.1.call-start = ((), (), s32[]{:S(2)}) async-start(), calls=%async_computation.9 | async-start | bytes 4194304 | tf_op jit(solution)/shard_map/psum | solution.py:126
  215.3 2.1 copy-start.2
  215.3 9.9 slice-start.2
  217.5 7.8 copy-start.19
  217.5 7.8 slice-start.3
  217.5 24.7 %slice-start = ((s8[8388608]{0:T(1024)(128)(4,1)}), s8[4194304]{0:T(1024)(128)(4,1)S(1)}, s32[]{:S(2)}) async-start(s8[8388608]{0:T(1024)(128)(4,1)} %bitcast.144), calls=%async_computation.17 | async-start | bytes 8388608
  225.3 15.5 %copy-start.14 = (f32[512,2048]{1,0:T(8,128)}, f32[512,2048]{1,0:T(8,128)S(1)}, u32[]{:S(2)}) copy-start(f32[512,2048]{1,0:T(8,128)S(1)} %fusion.81) | copy-start | bytes 12582916
  225.3 16.9 %slice-start.1 = ((s8[8388608]{0:T(1024)(128)(4,1)}), s8[4194304]{0:T(1024)(128)(4,1)S(1)}, s32[]{:S(2)}) async-start(s8[8388608]{0:T(1024)(128)(4,1)} %bitcast.144), calls=%async_computation.18 | async-start | bytes 8388608
  240.8 1.4 copy-start.36
  248.0 162.5 %reduce-scatter.7.cloned.1.call-start = ((), (), s32[]{:S(2)}) async-start(), calls=%async_computation.10 | async-start | bytes 5242880 | tf_op jit(solution)/shard_map/reduce_scatter | solution.py:161
  299.7 4.8 copy-start.3
  299.7 4.8 copy-start.10
  309.0 2.1 copy-start.7
  312.8 4.4 copy-start.13
  333.5 156.5 %reduce-scatter.9.cloned.1.call-start = ((), (), s32[]{:S(2)}) async-start(), calls=%async_computation.11 | async-start | bytes 5242880 | tf_op jit(solution)/shard_map/reduce_scatter | solution.py:164
  338.6 223.1 %reduce-scatter.13.cloned.1.call-start = ((), (), s32[]{:S(2)}) async-start(), calls=%async_computation.13 | async-start | bytes 2359296 | tf_op jit(solution)/shard_map/reduce_scatter | solution.py:193
  344.2 305.8 %all-reduce.10.cloned.1.call-start = ((), (), s32[]{:S(2)}) async-start(), calls=%async_computation.16 | async-start | bytes 8388608 | tf_op jit(solution)/shard_map/psum | solution.py:113
  349.0 1.3 copy-start.21
  350.3 9.2 copy-start.16
  491.6 7.6 copy-start.22
  499.3 1.6 copy-start.37
  499.3 304.0 %reduce-scatter.15.cloned.1.call-start = ((), (), s32[]{:S(2)}) async-start(), calls=%async_computation.14 | async-start | bytes 9437184 | tf_op jit(solution)/shard_map/reduce_scatter | solution.py:196
  510.4 1.6 copy-start.20
  510.4 444.4 %reduce-scatter.17.cloned.1.call-start = ((), (), s32[]{:S(2)}) async-start(), calls=%async_computation.15 | async-start | bytes 9437184 | tf_op jit(solution)/shard_map/reduce_scatter | solution.py:199
  520.3 1.6 copy-start.18
  520.4 555.9 %reduce-scatter.11.cloned.1.call-start = ((), (), s32[]{:S(2)}) async-start(), calls=%async_computation.12 | async-start | bytes 7077888 | tf_op jit(solution)/shard_map/reduce_scatter | solution.py:190
  528.3 123.6 %copy-start.5 = (bf16[4,128,2048]{2,1,0:T(8,128)(2,1)S(1)}, bf16[4,128,2048]{2,1,0:T(8,128)(2,1)}, u32[]{:S(2)}) copy-start(bf16[4,128,2048]{2,1,0:T(8,128)(2,1)} %param.12) | copy-start | bytes 6291460
  528.3 123.6 %copy-start.24 = (f32[1,2048]{1,0:T(1,128)S(1)}, f32[1,2048]{1,0:T(1,128)}, u32[]{:S(2)}) copy-start(f32[1,2048]{1,0:T(1,128)} %copy-done.23) | copy-start | bytes 24580
  528.3 123.6 %copy-start.26 = (f32[512]{0:T(512)S(1)}, f32[512]{0:T(512)}, u32[]{:S(2)}) copy-start(f32[512]{0:T(512)} %copy-done.25) | copy-start | bytes 6148
  528.3 123.6 %copy-start.28 = (f32[512]{0:T(512)S(1)}, f32[512]{0:T(512)}, u32[]{:S(2)}) copy-start(f32[512]{0:T(512)} %copy-done.27) | copy-start | bytes 6148
  698.0 5.1 copy-start.6
  698.0 5.5 copy-start.8
  698.0 6.4 copy-start.11
  704.4 374.4 %copy-start.1 = (bf16[2048,512]{1,0:T(8,128)(2,1)S(1)}, bf16[2048,512]{1,0:T(8,128)(2,1)}, u32[]{:S(2)}) copy-start(bf16[2048,512]{1,0:T(8,128)(2,1)} %param.16) | copy-start | bytes 6291460
Sparse Core Ops, SparseCore 0:
  20.3 48.9 all-gather.4
  71.4 44.1 all-gather.2
  127.6 84.1 all-reduce.5
  248.1 51.5 all-reduce.7
  333.6 76.8 reduce-scatter.6
  412.7 77.2 reduce-scatter.8
  493.6 68.0 reduce-scatter.12
  565.3 84.6 all-reduce.9
  654.0 149.1 reduce-scatter.14
  806.8 148.0 reduce-scatter.16
  958.9 117.3 reduce-scatter.10
where the time goes:
time: 1090 us
  waiting for transfers between devices  810 us (74%)
  matrix products  131 us (12%)
  other arithmetic  61.1 us (6%)
  blocking collectives  39.5 us (4%)
  local copies, waits for them, and re-layouts  28 us (3%)
  between operations  15 us (1%)
    reduce_scatter x1, waiting for transfers between devices, on_device(): lax.psum_scatter(grad_down_local.astype(jnp.bfloat16), ('dp', 'blk'), sca...  149 us
    reduce_scatter x1, waiting for transfers between devices, on_device(): lax.psum_scatter(grad_qkv_local.astype(jnp.bfloat16), ('dp', 'blk'), scat...  119 us
    reduce_scatter x1, waiting for transfers between devices, on_device(): lax.psum_scatter(grad_up_local.astype(jnp.bfloat16), ('dp', 'blk'), scatt...  95.8 us
    psum x1, waiting for transfers between devices, on_device(): lax.psum(contract_cols(gelu_low, w_down).astype(jnp.bfloat16), 'mp')  86.5 us
    psum x1, waiting for transfers between devices, on_device(): attn = lax.psum(contract_cols(mixed, w_out), 'mp') + biases[0]  80.3 us
    reduce_scatter x1, waiting for transfers between devices, on_device(): lax.psum_scatter(grad_values.reshape(items, full_len, width), 'blk', scat...  78 us
    psum x1, waiting for transfers between devices, on_device(): lax.psum(contract_cols(grad_upper, w_up).astype(jnp.bfloat16), 'mp')  51.4 us
    all_gather x1, waiting for transfers between devices, on_device(): lax.all_gather(keys_local, 'blk', axis=1, tiled=True)  43.1 us
  transfers between devices with their start and end apart: 11, of which 11 were waited for; matrix products, arithmetic and copies ran while one was open for 11% of the time, Pallas kernels for 0%

commit v1 on v0

v1 whole, which is shorter than its diff:
```python
import jax
import jax.numpy as jnp
from jax import lax
from jax.sharding import PartitionSpec as P

DH = 128
LOW = jnp.bfloat16
FULL = jnp.float32


def flip(size, bit):
    return [(i, i ^ bit) for i in range(size)]


def shift(size, step):
    return [(i, (i + step) % size) for i in range(size)]


def normalize(values):
    centered = values - jnp.mean(values, axis=-1, keepdims=True)
    variance = jnp.mean(centered * centered, axis=-1, keepdims=True)
    inverse = lax.rsqrt(variance + 1e-05)
    return centered * inverse, inverse


def norm_back(grad_norm, unit, inverse, gain):
    scaled = grad_norm * gain
    first = jnp.mean(scaled, axis=-1, keepdims=True)
    second = jnp.mean(scaled * unit, axis=-1, keepdims=True)
    return inverse * (scaled - first - unit * second)


def exact_gelu(values):
    return jax.nn.gelu(values, approximate=False)


def dot(left, right, dims):
    return lax.dot_general(left, right, (dims, ((), ())), preferred_element_type=FULL)


def on_device(
    dp,
    blk,
    mp,
    inputs,
    lengths,
    w_qkv,
    b_qv,
    w_out,
    out_biases,
    ln_gains,
    ln_shifts,
    w_up,
    b_up,
    w_down,
    cotangent,
):
    items, block_len, d_model = inputs.shape
    width = w_qkv.shape[2]
    heads = width // DH
    scale = DH ** (-0.5)
    sub = block_len // mp
    own_rows = blk * sub
    rows = own_rows * mp
    chunk = d_model // (dp * blk)
    x, z, me = lax.axis_index("dp"), lax.axis_index("blk"), lax.axis_index("mp")
    gains = ln_gains.astype(FULL)
    shifts = ln_shifts.astype(FULL)
    biases = out_biases.astype(FULL)

    def to_items(array):
        mine = lax.dynamic_slice_in_dim(array, me * sub, sub, axis=1)
        parts = [lax.dynamic_index_in_dim(mine, z, 0, keepdims=False)]
        for s in range(1, blk):
            piece = lax.dynamic_index_in_dim(mine, lax.rem(z + s, blk), 0, keepdims=False)
            parts.append(lax.ppermute(piece, "blk", shift(blk, s)))
        return jnp.concatenate(parts, axis=0)

    def gather_mp(own):
        half = jnp.concatenate([own, lax.ppermute(own, "mp", flip(mp, 2))], axis=0)
        return jnp.concatenate([half, lax.ppermute(half, "mp", flip(mp, 1))], axis=0)

    def scatter_mp(keep, send):
        keep = keep + lax.ppermute(send.astype(LOW), "mp", flip(mp, 1)).astype(FULL)
        got = lax.ppermute(keep[own_rows:].astype(LOW), "mp", flip(mp, 2))
        return keep[:own_rows] + got.astype(FULL)

    def from_items(own):
        parts = [own[:sub]]
        for s in range(1, blk):
            parts.append(lax.ppermute(own[s * sub : (s + 1) * sub], "blk", shift(blk, -s)))
        whole = gather_mp(jnp.concatenate(parts, axis=0)).reshape(mp, blk, sub, d_model)
        order = [0, 2, 1, 3]
        result = jnp.zeros((items, mp, sub, d_model), own.dtype)
        for at, j in enumerate(order):
            for s in range(blk):
                result = lax.dynamic_update_slice(
                    result, whole[at, s][None, None], (lax.rem(z + s, blk), me ^ j, 0, 0)
                )
        return result.reshape(items, block_len, d_model)

    in_block = jnp.arange(sub, dtype=jnp.int32)
    block_of = lax.rem(z - jnp.arange(blk, dtype=jnp.int32) + blk, blk)

    def positions_of(q):
        return (block_of[:, None] * block_len + q * sub + in_block[None, :]).reshape(-1)

    pos_own = positions_of(me)
    pos = jnp.concatenate([positions_of(me ^ j) for j in (0, 2, 1, 3)])
    length = lax.dynamic_index_in_dim(lengths, z, 0, keepdims=False)

    def ring_columns(array, parts):
        pieces = []
        for k in range(blk):
            at = lax.rem(z + k, blk)
            for part in parts:
                pieces.append(
                    lax.dynamic_slice_in_dim(array, (part * blk + at) * chunk, chunk, axis=1)
                )
        return jnp.concatenate(pieces, axis=1)

    def ring_scatter(partial):
        far = partial(2).astype(LOW)
        cut = far.shape[1] // 2
        from_left = lax.ppermute(far[:, :cut], "blk", shift(blk, 1))
        from_right = lax.ppermute(far[:, cut:], "blk", shift(blk, -1))
        right = partial(1)
        left = partial(3)
        right = jnp.concatenate([right[:, :cut] + from_left.astype(FULL), right[:, cut:]], axis=1)
        left = jnp.concatenate([left[:, :cut], left[:, cut:] + from_right.astype(FULL)], axis=1)
        from_left = lax.ppermute(right.astype(LOW), "blk", shift(blk, 1))
        from_right = lax.ppermute(left.astype(LOW), "blk", shift(blk, -1))
        return partial(0) + from_left.astype(FULL) + from_right.astype(FULL)

    other = [1 - x]

    def swap_dp(array):
        return lax.ppermute(array, "dp", flip(dp, 1))

    def all_columns(d_side):
        return ring_columns(d_side, list(range(dp)))

    def grad_all(d_cols, n_side):
        size = dp * chunk

        def partial(k):
            return dot(d_cols[:, k * size : (k + 1) * size], n_side, ((0,), (0,)))

        summed = ring_scatter(partial)
        if dp == 2:
            mine = lax.dynamic_slice_in_dim(summed, x * chunk, chunk, axis=0)
            theirs = lax.dynamic_slice_in_dim(summed, (1 - x) * chunk, chunk, axis=0)
            return mine + swap_dp(theirs.astype(LOW)).astype(FULL)
        return lax.psum_scatter(
            summed.astype(LOW), "dp", scatter_dimension=0, tiled=True
        ).astype(FULL)

    def grad_half(d_own, d_other, n_own):
        n_other = swap_dp(n_own)

        def partial(k):
            at = slice(k * chunk, (k + 1) * chunk)
            return dot(d_own[:, at], n_own, ((0,), (0,))) + dot(
                d_other[:, at], n_other, ((0,), (0,))
            )

        return ring_scatter(partial)

    def other_columns(own):
        return gather_mp(swap_dp(ring_columns(own, other)))

    def weight_grad(own, full, n_side):
        if dp == 2:
            return grad_half(ring_columns(full, [x]), other_columns(own), n_side)
        return grad_all(all_columns(full), n_side)

    x_own = to_items(inputs).astype(FULL)
    unit_one, inverse_one = normalize(x_own)
    act_one_own = (unit_one * gains[0] + shifts[0]).astype(LOW)
    act_one = gather_mp(act_one_own)
    qv_bias = b_qv.astype(FULL)

    def project(t):
        return dot(act_one, w_qkv[:, t], ((1,), (0,)))

    def by_head(array):
        return array.reshape(rows, heads, DH).transpose(1, 0, 2)

    queries = by_head((project(0) + qv_bias[0]).astype(LOW))
    keys = by_head(project(1).astype(LOW))
    values = by_head((project(2) + qv_bias[1]).astype(LOW))
    allowed = (pos[None, :] <= pos[:, None]) & (pos[None, :] < length)
    scores = jnp.einsum("nid,njd->nij", queries, keys, preferred_element_type=FULL)
    scores = jnp.where(allowed[None], scores * scale, -1e30)
    peak = jnp.max(scores, axis=-1, keepdims=True)
    expo = jnp.exp(scores - peak)
    probs = expo / jnp.sum(expo, axis=-1, keepdims=True)
    mixed = jnp.einsum("nij,njd->ind", probs.astype(LOW), values, preferred_element_type=FULL)
    mixed = mixed.reshape(rows, width).astype(LOW)
    half = rows // 2

    def halves(left, right, dims):
        return dot(left[:half], right, dims), dot(left[half:], right, dims)

    attn = scatter_mp(*halves(mixed, w_out, ((1,), (1,)))) + biases[0]
    resid = x_own + attn
    unit_two, inverse_two = normalize(resid)
    act_two_own = (unit_two * gains[1] + shifts[1]).astype(LOW)
    act_two = gather_mp(act_two_own)

    dy_own = to_items(cotangent).astype(FULL) * (pos_own < length).astype(FULL)[:, None]
    dy_own_low = dy_own.astype(LOW)
    dy = gather_mp(dy_own_low)

    upper = dot(act_two, w_up, ((1,), (0,))) + b_up.astype(FULL)
    gelu_vals, gelu_back = jax.vjp(exact_gelu, upper)
    gel = gelu_vals.astype(LOW)
    dup = gelu_back(dot(dy, w_down, ((1,), (0,))))[0].astype(LOW)
    da2 = scatter_mp(*halves(dup, w_up, ((1,), (1,))))
    dh = dy_own + norm_back(da2, unit_two, inverse_two, gains[1])
    dattn_own = dh.astype(LOW)
    dattn = gather_mp(dattn_own)
    dmixed = by_head(dot(dattn, w_out, ((1,), (0,))).astype(LOW))

    down = scatter_mp(*halves(gel, w_down, ((1,), (1,)))) + biases[1]
    output = from_items((resid + down).astype(LOW))

    dv = jnp.einsum("nij,nid->jnd", probs.astype(LOW), dmixed, preferred_element_type=FULL)
    dprobs = jnp.einsum("nid,njd->nij", dmixed, values, preferred_element_type=FULL)
    row_terms = jnp.sum(probs * dprobs, axis=-1, keepdims=True)
    dscores = (probs * (dprobs - row_terms) * scale).astype(LOW)
    dq = jnp.einsum("nij,njd->ind", dscores, keys, preferred_element_type=FULL)
    dk = jnp.einsum("nij,nid->jnd", dscores, queries, preferred_element_type=FULL)
    dqkv = [part.astype(LOW).reshape(rows, width) for part in (dq, dk, dv)]

    def da1_part(at):
        return sum(dot(dqkv[t][at], w_qkv[:, t], ((1,), (1,))) for t in range(3))

    da1 = scatter_mp(da1_part(slice(0, half)), da1_part(slice(half, rows)))
    input_grad = dh + norm_back(da1, unit_one, inverse_one, gains[0])
    input_grad = from_items(input_grad.astype(LOW)).astype(FULL)

    grad_down = weight_grad(dy_own_low, dy, gel)
    grad_up = weight_grad(act_two_own, act_two, dup)
    grad_out = grad_all(all_columns(dattn), mixed)
    grad_qkv = weight_grad(act_one_own, act_one, jnp.concatenate(dqkv, axis=1))
    grad_qkv = grad_qkv.reshape(chunk, 3, width)

    def sum_over(array, axis, size):
        bit = 1
        while bit < size:
            array = array + lax.ppermute(array, axis, flip(size, bit))
            bit *= 2
        return array

    def column_sum(array):
        return jnp.sum(array.astype(FULL), axis=0)

    def sum_groups(array):
        return sum_over(sum_over(array, "blk", blk), "dp", dp)

    first = jnp.concatenate(
        [column_sum(da2 * unit_two), column_sum(da2), column_sum(dattn_own), column_sum(dy_own)]
    )
    first = jnp.concatenate([sum_over(first, "mp", mp), column_sum(dup)])
    first = sum_groups(first)
    last = jnp.concatenate([column_sum(da1 * unit_one), column_sum(da1)])
    last = jnp.concatenate([sum_over(last, "mp", mp), column_sum(dqkv[0]), column_sum(dqkv[2])])
    last = sum_groups(last)
    gain_two, shift_two, attn_bias, down_bias = [
        first[i * d_model : (i + 1) * d_model] for i in range(4)
    ]
    grad_up_bias = first[4 * d_model :]
    gain_one, shift_one = last[:d_model], last[d_model : 2 * d_model]
    grad_qv_bias = last[2 * d_model :].reshape(2, width)
    return (
        output,
        input_grad,
        grad_qkv,
        grad_qv_bias,
        grad_out,
        jnp.stack([attn_bias, down_bias]),
        jnp.stack([gain_one, gain_two]),
        jnp.stack([shift_one, shift_two]),
        grad_up,
        grad_up_bias,
        grad_down,
    )


def solution(mesh):
    sizes = [mesh.shape[name] for name in ("dp", "blk", "mp")]
    in_specs = (
        P("dp", "blk", None),
        P("dp"),
        P(None, None, "mp"),
        P(None, "mp"),
        P(None, "mp"),
        P(),
        P(),
        P(),
        P(None, "mp"),
        P("mp"),
        P(None, "mp"),
        P("dp", "blk", None),
    )
    out_specs = (
        P("dp", "blk", None),
        P("dp", "blk", None),
        P(("dp", "blk"), None, "mp"),
        P(None, "mp"),
        P(("dp", "blk"), "mp"),
        P(),
        P(),
        P(),
        P(("dp", "blk"), "mp"),
        P("mp"),
        P(("dp", "blk"), "mp"),
    )

    def step(*arrays):
        return on_device(*sizes, *arrays)

    return jax.shard_map(
        step, mesh=mesh, in_specs=in_specs, out_specs=out_specs, check_vma=False
    )
```

time: 1090 us -> 595 us (0.55)
  waiting for transfers between devices: 810 us -> 295 us
  starting transfers between devices: 1.56 us -> 68.2 us
  blocking collectives: 39.5 us -> 0 us
  other arithmetic: 61.1 us -> 33.8 us
  matrix products: 131 us -> 148 us
  between operations: 15 us -> 2.83 us
    reduce_scatter x6 -> x0, waiting for transfers between devices: 508 us -> none  [the longest x1 149 us: on_device(): lax.psum_scatter(grad_down_local.astype(jnp.bfloat16), ('dp', 'blk'), sca...]
    ppermute x0 -> x71, waiting for transfers between devices: none -> 295 us  [the longest x10 77.7 us: sum_over(): array = array + lax.ppermute(array, axis, flip(size, bit))]
    psum x3 -> x0, waiting for transfers between devices: 218 us -> none  [the longest x1 86.5 us: on_device(): lax.psum(contract_cols(gelu_low, w_down).astype(jnp.bfloat16), 'mp')]
    all_gather x2 -> x0, waiting for transfers between devices: 83.5 us -> none  [the longest x1 43.1 us: on_device(): lax.all_gather(keys_local, 'blk', axis=1, tiled=True)]
    ppermute x0 -> x71, starting transfers between devices: none -> 68.2 us  [the longest x6 10.8 us: to_items(): parts.append(lax.ppermute(piece, 'blk', shift(blk, s)))]
    psum x1 -> x0, blocking collectives: 39.5 us -> none  [on_device(): lax.psum(qv_bias_grad.astype(jnp.bfloat16), ('dp', 'blk'))]
    convert_element_type x17 -> x6, other arithmetic: 28.9 us -> 5.15 us  [the longest x2 3.26 us: on_device(): input_grad = from_items(input_grad.astype(LOW)).astype(FULL)]
    reduce_sum x11 -> x8, other arithmetic: 28.7 us -> 5.96 us  [the longest x4 4.94 us: column_sum(): return jnp.sum(array.astype(FULL), axis=0)]
  transfers between devices with their start and end apart: 11 -> 71, of which waited for: 11 -> 33; matrix products, arithmetic and copies ran while one was open for 11% -> 32% of each run, Pallas kernels for 0% -> 0%
where the time goes in v1:
time: 595 us; the launch traced here: 587 us
  waiting for transfers between devices  295 us (50%)
  matrix products  148 us (25%)
  starting transfers between devices  68.2 us (11%)
  local copies, waits for them, and re-layouts  38.7 us (7%)
  other arithmetic  33.8 us (6%)
    dot_general x46, matrix products, dot(): lax.dot_general(left, right, (dims, ((), ())), preferred_element_type=FULL)  120 us
    ppermute x10, waiting for transfers between devices, sum_over(): array = array + lax.ppermute(array, axis, flip(size, bit))  77.7 us
    ppermute x4, waiting for transfers between devices, ring_scatter(): from_left = lax.ppermute(right.astype(LOW), 'blk', shift(blk, 1))  48 us
    ppermute x9, waiting for transfers between devices, gather_mp(): half = jnp.concatenate([own, lax.ppermute(own, 'mp', flip(mp, 2))], axis=0)  39.3 us
    ppermute x4, waiting for transfers between devices, ring_scatter(): from_right = lax.ppermute(left.astype(LOW), 'blk', shift(blk, -1))  32.9 us
    ppermute x4, waiting for transfers between devices, scatter_mp(): got = lax.ppermute(keep[own_rows:].astype(LOW), 'mp', flip(mp, 2))  24.7 us
    ppermute x4, waiting for transfers between devices, ring_scatter(): from_left = lax.ppermute(far[:, :cut], 'blk', shift(blk, 1))  22.1 us
    ppermute x4, waiting for transfers between devices, ring_scatter(): from_right = lax.ppermute(far[:, cut:], 'blk', shift(blk, -1))  17.2 us
  transfers between devices with their start and end apart: 71, of which 33 were waited for; matrix products, arithmetic and copies ran while one was open for 32% of the time, Pallas kernels for 0%

profile of v1, /device:TPU:0, one launch (start us, length us, event | category | flops | bytes accessed | tf_op | source)
XLA Modules:
  0.0 586.9 jit_solution(17032404317059223965)
XLA Ops:
  2.1 5.1 collective-permute-start.2
  11.2 7.3 %collective-permute-done.1 = bf16[32,2048]{1,0:T(8,128)(2,1)S(1)} collective-permute-done((bf16[32,2048]{1,0:T(8,128)(2,1)S(1)}, bf16[32,2048]{1,0:T(8,128)(2,1)S(1)}, u32[]{:S(2)}, u32[]{:S(2)}) %collective-permute-start.1) | collective-permute-done | bytes 131104 | tf_op jit(solution)/shard_map/ppermute | solution.py:76
  21.0 11.6 %collective-permute-done.3 = bf16[128,2048]{1,0:T(8,128)(2,1)S(1)} collective-permute-done((bf16[128,2048]{1,0:T(8,128)(2,1)S(1)}, bf16[128,2048]{1,0:T(8,128)(2,1)S(1)}, u32[]{:S(2)}, u32[]{:S(2)}) %collective-permute-start.3) | collective-permute-done | bytes 524320 | tf_op jit(solution)/shard_map/ppermute | solution.py:80
  36.8 4.2 fusion.64
  41.0 4.0 fusion.67
  45.0 5.6 fusion.223
  50.6 3.3 fusion.70
  62.0 2.2 collective-permute-start.16
  67.1 7.6 %collective-permute-done.17 = bf16[32,2048]{1,0:T(8,128)(2,1)} collective-permute-done((bf16[32,2048]{1,0:T(8,128)(2,1)}, bf16[32,2048]{1,0:T(8,128)(2,1)}, u32[]{:S(2)}, u32[]{:S(2)}) %collective-permute-start.17) | collective-permute-done | bytes 131104 | tf_op jit(solution)/shard_map/ppermute | solution.py:76
  86.9 7.7 %collective-permute-done.6 = bf16[128,2048]{1,0:T(8,128)(2,1)S(1)} collective-permute-done((bf16[128,2048]{1,0:T(8,128)(2,1)S(1)}, bf16[128,2048]{1,0:T(8,128)(2,1)S(1)}, u32[]{:S(2)}, u32[]{:S(2)}) %collective-permute-start.6) | collective-permute-done | bytes 524320 | tf_op jit(solution)/shard_map/ppermute | solution.py:85
  97.0 8.8 %collective-permute-done.19 = bf16[128,2048]{1,0:T(8,128)(2,1)S(1)} collective-permute-done((bf16[128,2048]{1,0:T(8,128)(2,1)S(1)}, bf16[128,2048]{1,0:T(8,128)(2,1)S(1)}, u32[]{:S(2)}, u32[]{:S(2)}) %collective-permute-start.19) | collective-permute-done | bytes 524320 | tf_op jit(solution)/shard_map/ppermute | solution.py:80
  106.9 4.5 collective-permute-done.33
  111.6 5.5 collective-permute-done.64
  117.9 8.9 %collective-permute-done.7 = bf16[128,2048]{1,0:T(8,128)(2,1)S(1)} collective-permute-done((bf16[128,2048]{1,0:T(8,128)(2,1)S(1)}, bf16[128,2048]{1,0:T(8,128)(2,1)S(1)}, u32[]{:S(2)}, u32[]{:S(2)}) %collective-permute-start.7) | collective-permute-done | bytes 524320 | tf_op jit(solution)/shard_map/ppermute | solution.py:80
  130.4 2.1 copy.37
  132.5 3.2 pad_maximum_fusion
  137.8 6.8 %collective-permute-done.55 = bf16[128,1024]{1,0:T(8,128)(2,1)S(1)} collective-permute-done((bf16[128,1024]{1,0:T(8,128)(2,1)S(1)}, bf16[128,1024]{1,0:T(8,128)(2,1)S(1)}, u32[]{:S(2)}, u32[]{:S(2)}) %collective-permute-start.55) | collective-permute-done | bytes 262176 | tf_op jit(solution)/shard_map/ppermute | solution.py:138
  146.0 17.3 %multiply_convert_fusion.1 = (bf16[512,2048]{1,0:T(8,128)(2,1)S(1)}, f32[512,2048]{1,0:T(8,128)S(1)}, f32[512,2048]{1,0:T(8,128)S(1)}) fusion(f32[2048]{0:T(1024)S(1)} %copy-done.60, bf16[2048,2048]{1,0:T(8,128)(2,1)} %param.20, bf16[256,2048]{1,0:T(8,128)(2,1)} %collective-permute-done.8, bf16[128,2048]{1,0:T(8,128)(2,1)S(1)} %copy-done.40, ...), kind=kOutput, calls=%fused_computation.9 | convolution fusion | flops 4370464768 | bytes 20979712 | tf_op jit(solution)/shard_map/dot_general | solution.py:38
  163.3 10.3 %convert_reduce_fusion = (f32[2048]{0:T(1024)S(1)}, bf16[512,2048]{1,0:T(8,128)(2,1)S(1)}) fusion(f32[512,2048]{1,0:T(8,128)S(1)} %get-tuple-element.45, bf16[2048,2048]{1,0:T(8,128)(2,1)} %param.22, bf16[256,2048]{1,0:T(8,128)(2,1)} %collective-permute-done.20, bf16[128,2048]{1,0:T(8,128)(2,1)S(1)} %copy-done.42, bf16[128,2048]{1,0:T(8,128)(2,1)S(1)} %copy-done.15, ...), kind=kOutput, calls=%fused_computation.4 | convolution fusion | flops 4319082496 | bytes 20987904 | tf_op jit(solution)/shard_map/dot_general | solution.py:38
  173.6 6.5 %convolution_convert_fusion.1 = bf16[256,2048]{1,0:T(8,128)(2,1)S(1)} fusion(bf16[2048,2048]{1,0:T(8,128)(2,1)} %param.20, bf16[512,2048]{1,0:T(8,128)(2,1)S(1)} %get-tuple-element.146), kind=kOutput, calls=%fused_computation.53 | convolution fusion | flops 2148007936 | bytes 10485760 | tf_op jit(solution)/shard_map/dot_general | solution.py:38
  180.2 5.9 %convolution_convert_fusion.2 = bf16[256,2048]{1,0:T(8,128)(2,1)S(1)} fusion(bf16[2048,2048]{1,0:T(8,128)(2,1)} %param.22, bf16[512,2048]{1,0:T(8,128)(2,1)S(1)} %get-tuple-element.44), kind=kOutput, calls=%fused_computation.54 | convolution fusion | flops 2148007936 | bytes 10485760 | tf_op jit(solution)/shard_map/dot_general | solution.py:38
  186.9 5.7 convert_add_fusion.1
  193.5 5.8 convert_add_fusion.2
  200.8 6.7 %collective-permute-done.22 = bf16[128,2048]{1,0:T(8,128)(2,1)S(1)} collective-permute-done((bf16[128,2048]{1,0:T(8,128)(2,1)S(1)}, bf16[128,2048]{1,0:T(8,128)(2,1)S(1)}, u32[]{:S(2)}, u32[]{:S(2)}) %collective-permute-start.22) | collective-permute-done | bytes 524320 | tf_op jit(solution)/shard_map/ppermute | solution.py:85
  208.0 10.3 %collective-permute-done.10 = bf16[128,2048]{1,0:T(8,128)(2,1)S(1)} collective-permute-done((bf16[128,2048]{1,0:T(8,128)(2,1)S(1)}, bf16[128,2048]{1,0:T(8,128)(2,1)S(1)}, u32[]{:S(2)}, u32[]{:S(2)}) %collective-permute-start.10) | collective-permute-done | bytes 524320 | tf_op jit(solution)/shard_map/ppermute | solution.py:85
  218.4 2.7 convert_reduce_fusion.2
  228.1 2.4 collective-permute-start.11
  231.6 2.8 collective-permute-done.11
  235.1 7.5 %collective-permute-done.12 = bf16[32,2048]{1,0:T(8,128)(2,1)S(1)} collective-permute-done((bf16[32,2048]{1,0:T(8,128)(2,1)S(1)}, bf16[32,2048]{1,0:T(8,128)(2,1)S(1)}, u32[]{:S(2)}, u32[]{:S(2)}) %collective-permute-start.12) | collective-permute-done | bytes 131104 | tf_op jit(solution)/shard_map/ppermute | solution.py:91
  244.7 2.8 collective-permute-done.53
  248.7 66.4 %collective-permute-done.54 = f32[10240]{0:T(1024)S(1)} collective-permute-done((f32[10240]{0:T(1024)S(1)}, f32[10240]{0:T(1024)S(1)}, u32[]{:S(2)}, u32[]{:S(2)}) %collective-permute-start.54) | collective-permute-done | bytes 40992 | tf_op jit(solution)/shard_map/ppermute | solution.py:252
  335.2 3.0 fusion.145
  341.0 3.8 collective-permute-done.59
  347.5 8.4 %collective-permute-done.69 = bf16[256,1024]{1,0:T(8,128)(2,1)S(1)} collective-permute-done((bf16[256,1024]{1,0:T(8,128)(2,1)S(1)}, bf16[256,1024]{1,0:T(8,128)(2,1)S(1)}, u32[]{:S(2)}, u32[]{:S(2)}) %collective-permute-start.69) | collective-permute-done | bytes 524320 | tf_op jit(solution)/shard_map/ppermute | solution.py:126
  357.7 9.6 %collective-permute-done.67 = bf16[256,1024]{1,0:T(8,128)(2,1)S(1)} collective-permute-done((bf16[256,1024]{1,0:T(8,128)(2,1)S(1)}, bf16[256,1024]{1,0:T(8,128)(2,1)S(1)}, u32[]{:S(2)}, u32[]{:S(2)}) %collective-permute-start.67) | collective-permute-done | bytes 524320 | tf_op jit(solution)/shard_map/ppermute | solution.py:125
  370.6 2.7 fusion.135
  373.3 8.1 %convert_reduce_fusion.4 = (f32[4,128]{1,0:T(4,128)S(1)}, bf16[4,128,512]{2,1,0:T(8,128)(2,1)S(1)}) fusion(bf16[4,512,128]{1,2,0:T(8,128)(2,1)S(1)} %bitcast.256, f32[4,512,512]{1,2,0:T(8,128)} %fusion.135, f32[4,512,512]{1,2,0:T(8,128)} %get-tuple-element.139, f32[4,512]{1,0:T(4,128)S(1)} %copy-done.71), kind=kOutput, calls=%fused_computation.167 | convolution fusion | flops 276563968 | bytes 9447424 | tf_op jit(solution)/shard_map/nij,njd->ind/dot_general | solution.py:232
  381.4 7.9 %fusion.76 = bf16[4,128,512]{2,1,0:T(8,128)(2,1)S(1)} fusion(bf16[4,512,128]{1,2,0:T(8,128)(2,1)} %bitcast.254, f32[4,512,512]{1,2,0:T(8,128)} %fusion.135, f32[4,512,512]{1,2,0:T(8,128)} %get-tuple-element.139, f32[4,512]{1,0:T(4,128)S(1)} %copy-done.71), kind=kOutput, calls=%fused_computation.109 | convolution fusion | flops 276040192 | bytes 9445376 | tf_op jit(solution)/shard_map/nij,nid->jnd/dot_general | solution.py:233
  389.3 3.3 convert_reduce_fusion.3
  392.7 2.5 fusion.32
  395.3 2.4 convolution_add_fusion.13
  397.7 2.5 fusion.18
  409.1 8.8 %collective-permute-done.47 = bf16[512,256]{1,0:T(8,128)(2,1)S(1)} collective-permute-done((bf16[512,256]{1,0:T(8,128)(2,1)S(1)}, bf16[512,256]{1,0:T(8,128)(2,1)S(1)}, u32[]{:S(2)}, u32[]{:S(2)}) %collective-permute-start.47) | collective-permute-done | bytes 262176 | tf_op jit(solution)/shard_map/ppermute | solution.py:126
  419.6 3.9 collective-permute-done.45
  423.8 3.9 collective-permute-start.70
  427.7 3.9 fusion.16
  431.6 3.2 collective-permute-done.48
  435.4 10.7 %collective-permute-done.46 = bf16[512,512]{1,0:T(8,128)(2,1)S(1)} collective-permute-done((bf16[512,512]{1,0:T(8,128)(2,1)S(1)}, bf16[512,512]{1,0:T(8,128)(2,1)S(1)}, u32[]{:S(2)}, u32[]{:S(2)}) %collective-permute-start.46) | collective-permute-done | bytes 524320 | tf_op jit(solution)/shard_map/ppermute | solution.py:131
  448.6 19.8 %collective-permute-done.70 = bf16[256,2048]{1,0:T(8,128)(2,1)S(1)} collective-permute-done((bf16[256,2048]{1,0:T(8,128)(2,1)S(1)}, bf16[256,2048]{1,0:T(8,128)(2,1)S(1)}, u32[]{:S(2)}, u32[]{:S(2)}) %collective-permute-start.70) | collective-permute-done | bytes 1048608 | tf_op jit(solution)/shard_map/ppermute | solution.py:132
  468.4 22.2 %collective-permute-done.68 = bf16[256,2048]{1,0:T(8,128)(2,1)S(1)} collective-permute-done((bf16[256,2048]{1,0:T(8,128)(2,1)S(1)}, bf16[256,2048]{1,0:T(8,128)(2,1)S(1)}, u32[]{:S(2)}, u32[]{:S(2)}) %collective-permute-start.68) | collective-permute-done | bytes 1048608 | tf_op jit(solution)/shard_map/ppermute | solution.py:131
  490.6 3.2 fusion.17
  506.6 3.0 collective-permute-start.38
  509.6 2.4 collective-permute-start.42
  513.6 5.5 collective-permute-done.42
  523.8 2.1 collective-permute-start.36
  532.9 4.9 collective-permute-done.36
  539.9 2.9 fusion.161
  544.7 9.9 %collective-permute-done.39 = bf16[256,1536]{1,0:T(8,128)(2,1)} collective-permute-done((bf16[256,1536]{1,0:T(8,128)(2,1)}, bf16[256,1536]{1,0:T(8,128)(2,1)}, u32[]{:S(2)}, u32[]{:S(2)}) %collective-permute-start.39) | collective-permute-done | bytes 786464 | tf_op jit(solution)/shard_map/ppermute | solution.py:132
  554.6 15.1 %collective-permute-done.37 = bf16[256,1536]{1,0:T(8,128)(2,1)} collective-permute-done((bf16[256,1536]{1,0:T(8,128)(2,1)}, bf16[256,1536]{1,0:T(8,128)(2,1)}, u32[]{:S(2)}, u32[]{:S(2)}) %collective-permute-start.37) | collective-permute-done | bytes 786464 | tf_op jit(solution)/shard_map/ppermute | solution.py:131
  569.8 3.9 fusion.13
  573.7 3.0 copy.46
  576.7 3.0 copy.51
  579.7 2.3 constant_dynamic-update-slice_fusion.17
  584.0 2.7 bitcast_convert_fusion
  (464 shorter events, 138.1 us)
Async XLA Ops:
  2.1 9.0 %collective-permute-start.2 = (bf16[32,2048]{1,0:T(8,128)(2,1)S(1)}, bf16[32,2048]{1,0:T(8,128)(2,1)S(1)}, u32[]{:S(2)}, u32[]{:S(2)}) collective-permute-start(bf16[32,2048]{1,0:T(8,128)(2,1)S(1)} %get-tuple-element.62), channel_id=1, source_target_pairs={{0,12},{4,0},{8,4},{12,8},{1,13},{5,1},{9,5},{13,9},{2,14},{6,2},{... | collective-permute-start | bytes 393224 | tf_op jit(solution)/shard_map/ppermute | solution.py:76
  7.3 11.2 %collective-permute-start.1 = (bf16[32,2048]{1,0:T(8,128)(2,1)S(1)}, bf16[32,2048]{1,0:T(8,128)(2,1)S(1)}, u32[]{:S(2)}, u32[]{:S(2)}) collective-permute-start(bf16[32,2048]{1,0:T(8,128)(2,1)S(1)} %get-tuple-element.63), channel_id=1, source_target_pairs={{0,8},{4,12},{8,0},{12,4},{1,9},{5,13},{9,1},{13,5},{2,10},{6,14},... | collective-permute-start | bytes 393224 | tf_op jit(solution)/shard_map/ppermute | solution.py:76
  7.3 11.2 %collective-permute-start = (bf16[32,2048]{1,0:T(8,128)(2,1)S(1)}, bf16[32,2048]{1,0:T(8,128)(2,1)S(1)}, u32[]{:S(2)}, u32[]{:S(2)}) collective-permute-start(bf16[32,2048]{1,0:T(8,128)(2,1)S(1)} %get-tuple-element.61), channel_id=1, source_target_pairs={{0,4},{4,8},{8,12},{12,0},{1,5},{5,9},{9,13},{13,1},{2,6},{6,10},{... | collective-permute-start | bytes 393224 | tf_op jit(solution)/shard_map/ppermute | solution.py:76
  19.4 13.2 %collective-permute-start.3 = (bf16[128,2048]{1,0:T(8,128)(2,1)S(1)}, bf16[128,2048]{1,0:T(8,128)(2,1)S(1)}, u32[]{:S(2)}, u32[]{:S(2)}) collective-permute-start(bf16[128,2048]{1,0:T(8,128)(2,1)S(1)} %fusion.86), channel_id=1, source_target_pairs={{0,2},{1,3},{2,0},{3,1},{4,6},{5,7},{6,4},{7,5},{8,10},{9,11},{10,... | collective-permute-start | bytes 1572872 | tf_op jit(solution)/shard_map/ppermute | solution.py:80
  57.3 20.2 %collective-permute-start.5 = (bf16[256,2048]{1,0:T(8,128)(2,1)}, bf16[256,2048]{1,0:T(8,128)(2,1)}, u32[]{:S(2)}, u32[]{:S(2)}) collective-permute-start(bf16[256,2048]{1,0:T(8,128)(2,1)} %convolution_convert_fusion), channel_id=1, source_target_pairs={{0,1},{1,0},{2,3},{3,2},{4,5},{5,4},{6,7},{7,6},{8,9},{9,8},{10,11... | collective-permute-start | bytes 3145736 | tf_op jit(solution)/shard_map/ppermute | solution.py:84
  59.5 7.6 %collective-permute-start.18 = (bf16[32,2048]{1,0:T(8,128)(2,1)}, bf16[32,2048]{1,0:T(8,128)(2,1)S(1)}, u32[]{:S(2)}, u32[]{:S(2)}) collective-permute-start(bf16[32,2048]{1,0:T(8,128)(2,1)} %get-tuple-element.58), channel_id=1, source_target_pairs={{0,12},{4,0},{8,4},{12,8},{1,13},{5,1},{9,5},{13,9},{2,14},{6,2},{... | collective-permute-start | bytes 393224 | tf_op jit(solution)/shard_map/ppermute | solution.py:76
  60.1 14.6 %collective-permute-start.17 = (bf16[32,2048]{1,0:T(8,128)(2,1)}, bf16[32,2048]{1,0:T(8,128)(2,1)}, u32[]{:S(2)}, u32[]{:S(2)}) collective-permute-start(bf16[32,2048]{1,0:T(8,128)(2,1)} %get-tuple-element.59), channel_id=1, source_target_pairs={{0,8},{4,12},{8,0},{12,4},{1,9},{5,13},{9,1},{13,5},{2,10},{6,14},... | collective-permute-start | bytes 393224 | tf_op jit(solution)/shard_map/ppermute | solution.py:76
  62.0 12.7 %collective-permute-start.16 = (bf16[32,2048]{1,0:T(8,128)(2,1)}, bf16[32,2048]{1,0:T(8,128)(2,1)}, u32[]{:S(2)}, u32[]{:S(2)}) collective-permute-start(bf16[32,2048]{1,0:T(8,128)(2,1)} %get-tuple-element.57), channel_id=1, source_target_pairs={{0,4},{4,8},{8,12},{12,0},{1,5},{5,9},{9,13},{13,1},{2,6},{6,10},{... | collective-permute-start | bytes 393224 | tf_op jit(solution)/shard_map/ppermute | solution.py:76
  65.6 16.8 %collective-permute-start.32 = (bf16[128,1024]{1,0:T(8,128)(2,1)S(1)}, bf16[128,1024]{1,0:T(8,128)(2,1)S(1)}, u32[]{:S(2)}, u32[]{:S(2)}) collective-permute-start(bf16[128,1024]{1,0:T(8,128)(2,1)S(1)} %pad_maximum_fusion.24), channel_id=1, source_target_pairs={{0,16},{16,0},{1,17},{17,1},{2,18},{18,2},{3,19},{19,3},{4,20},{20... | collective-permute-start | bytes 786440 | tf_op jit(solution)/shard_map/ppermute | solution.py:138
  76.0 8.0 %collective-permute-start.63 = (bf16[128,1024]{1,0:T(8,128)(2,1)S(1)}, bf16[128,1024]{1,0:T(8,128)(2,1)S(1)}, u32[]{:S(2)}, u32[]{:S(2)}) collective-permute-start(bf16[128,1024]{1,0:T(8,128)(2,1)S(1)} %pad_maximum_fusion.26), channel_id=1, source_target_pairs={{0,16},{16,0},{1,17},{17,1},{2,18},{18,2},{3,19},{19,3},{4,20},{20... | collective-permute-start | bytes 786440 | tf_op jit(solution)/shard_map/ppermute | solution.py:138
  79.7 14.9 %collective-permute-start.6 = (bf16[128,2048]{1,0:T(8,128)(2,1)S(1)}, bf16[128,2048]{1,0:T(8,128)(2,1)S(1)}, u32[]{:S(2)}, u32[]{:S(2)}) collective-permute-start(bf16[128,2048]{1,0:T(8,128)(2,1)S(1)} %slice.840), channel_id=1, source_target_pairs={{0,2},{1,3},{2,0},{3,1},{4,6},{5,7},{6,4},{7,5},{8,10},{9,11},{10,... | collective-permute-start | bytes 1572872 | tf_op jit(solution)/shard_map/ppermute | solution.py:85
  81.7 24.1 %collective-permute-start.19 = (bf16[128,2048]{1,0:T(8,128)(2,1)S(1)}, bf16[128,2048]{1,0:T(8,128)(2,1)S(1)}, u32[]{:S(2)}, u32[]{:S(2)}) collective-permute-start(bf16[128,2048]{1,0:T(8,128)(2,1)S(1)} %get-tuple-element.72), channel_id=1, source_target_pairs={{0,2},{1,3},{2,0},{3,1},{4,6},{5,7},{6,4},{7,5},{8,10},{9,11},{10,... | collective-permute-start | bytes 1572872 | tf_op jit(solution)/shard_map/ppermute | solution.py:80
  82.4 29.0 %collective-permute-start.33 = (bf16[128,1024]{1,0:T(8,128)(2,1)S(1)}, bf16[128,1024]{1,0:T(8,128)(2,1)S(1)}, u32[]{:S(2)}, u32[]{:S(2)}) collective-permute-start(bf16[128,1024]{1,0:T(8,128)(2,1)S(1)} %collective-permute-done.32), channel_id=1, source_target_pairs={{0,2},{1,3},{2,0},{3,1},{4,6},{5,7},{6,4},{7,5},{8,10},{9,11},{10,... | collective-permute-start | bytes 786440 | tf_op jit(solution)/shard_map/ppermute | solution.py:80
  84.1 33.0 %collective-permute-start.64 = (bf16[128,1024]{1,0:T(8,128)(2,1)S(1)}, bf16[128,1024]{1,0:T(8,128)(2,1)S(1)}, u32[]{:S(2)}, u32[]{:S(2)}) collective-permute-start(bf16[128,1024]{1,0:T(8,128)(2,1)S(1)} %collective-permute-done.63), channel_id=1, source_target_pairs={{0,2},{1,3},{2,0},{3,1},{4,6},{5,7},{6,4},{7,5},{8,10},{9,11},{10,... | collective-permute-start | bytes 786440 | tf_op jit(solution)/shard_map/ppermute | solution.py:80
  95.6 31.3 %collective-permute-start.7 = (bf16[128,2048]{1,0:T(8,128)(2,1)S(1)}, bf16[128,2048]{1,0:T(8,128)(2,1)S(1)}, u32[]{:S(2)}, u32[]{:S(2)}) collective-permute-start(bf16[128,2048]{1,0:T(8,128)(2,1)S(1)} %add_convert_fusion.1), channel_id=1, source_target_pairs={{0,2},{1,3},{2,0},{3,1},{4,6},{5,7},{6,4},{7,5},{8,10},{9,11},{10,... | collective-permute-start | bytes 1572872 | tf_op jit(solution)/shard_map/ppermute | solution.py:80
  106.9 29.5 %collective-permute-start.20 = (bf16[256,2048]{1,0:T(8,128)(2,1)}, bf16[256,2048]{1,0:T(8,128)(2,1)}, u32[]{:S(2)}, u32[]{:S(2)}) collective-permute-start(bf16[256,2048]{1,0:T(8,128)(2,1)} %pad_maximum_fusion.7), channel_id=1, source_target_pairs={{0,1},{1,0},{2,3},{3,2},{4,5},{5,4},{6,7},{7,6},{8,9},{9,8},{10,11... | collective-permute-start | bytes 3145736 | tf_op jit(solution)/shard_map/ppermute | solution.py:81
  111.5 17.2 %collective-permute-start.34 = (bf16[256,1024]{1,0:T(8,128)(2,1)S(1)}, bf16[256,1024]{1,0:T(8,128)(2,1)S(1)}, u32[]{:S(2)}, u32[]{:S(2)}) collective-permute-start(bf16[256,1024]{1,0:T(8,128)(2,1)S(1)} %pad_maximum_fusion.19), channel_id=1, source_target_pairs={{0,1},{1,0},{2,3},{3,2},{4,5},{5,4},{6,7},{7,6},{8,9},{9,8},{10,11... | collective-permute-start | bytes 1572872 | tf_op jit(solution)/shard_map/ppermute | solution.py:81
  117.1 12.5 %collective-permute-start.65 = (bf16[256,1024]{1,0:T(8,128)(2,1)S(1)}, bf16[256,1024]{1,0:T(8,128)(2,1)S(1)}, u32[]{:S(2)}, u32[]{:S(2)}) collective-permute-start(bf16[256,1024]{1,0:T(8,128)(2,1)S(1)} %pad_maximum_fusion.23), channel_id=1, source_target_pairs={{0,1},{1,0},{2,3},{3,2},{4,5},{5,4},{6,7},{7,6},{8,9},{9,8},{10,11... | collective-permute-start | bytes 1572872 | tf_op jit(solution)/shard_map/ppermute | solution.py:81
  128.0 18.0 %collective-permute-start.8 = (bf16[256,2048]{1,0:T(8,128)(2,1)}, bf16[256,2048]{1,0:T(8,128)(2,1)}, u32[]{:S(2)}, u32[]{:S(2)}) collective-permute-start(bf16[256,2048]{1,0:T(8,128)(2,1)} %pad_maximum_fusion.6), channel_id=1, source_target_pairs={{0,1},{1,0},{2,3},{3,2},{4,5},{5,4},{6,7},{7,6},{8,9},{9,8},{10,11... | collective-permute-start | bytes 3145736 | tf_op jit(solution)/shard_map/ppermute | solution.py:81
  135.9 8.8 %collective-permute-start.55 = (bf16[128,1024]{1,0:T(8,128)(2,1)S(1)}, bf16[128,1024]{1,0:T(8,128)(2,1)S(1)}, u32[]{:S(2)}, u32[]{:S(2)}) collective-permute-start(bf16[128,1024]{1,0:T(8,128)(2,1)S(1)} %pad_maximum_fusion.25), channel_id=1, source_target_pairs={{0,16},{16,0},{1,17},{17,1},{2,18},{18,2},{3,19},{19,3},{4,20},{20... | collective-permute-start | bytes 786440 | tf_op jit(solution)/shard_map/ppermute | solution.py:138
  144.6 42.1 %collective-permute-start.56 = (bf16[128,1024]{1,0:T(8,128)(2,1)S(1)}, bf16[128,1024]{1,0:T(8,128)(2,1)S(1)}, u32[]{:S(2)}, u32[]{:S(2)}) collective-permute-start(bf16[128,1024]{1,0:T(8,128)(2,1)S(1)} %collective-permute-done.55), channel_id=1, source_target_pairs={{0,2},{1,3},{2,0},{3,1},{4,6},{5,7},{6,4},{7,5},{8,10},{9,11},{10,... | collective-permute-start | bytes 786440 | tf_op jit(solution)/shard_map/ppermute | solution.py:80
  180.1 6.8 %collective-permute-start.21 = (bf16[256,2048]{1,0:T(8,128)(2,1)S(1)}, bf16[256,2048]{1,0:T(8,128)(2,1)S(1)}, u32[]{:S(2)}, u32[]{:S(2)}) collective-permute-start(bf16[256,2048]{1,0:T(8,128)(2,1)S(1)} %convolution_convert_fusion.1), channel_id=1, source_target_pairs={{0,1},{1,0},{2,3},{3,2},{4,5},{5,4},{6,7},{7,6},{8,9},{9,8},{10,11... | collective-permute-start | bytes 3145736 | tf_op jit(solution)/shard_map/ppermute | solution.py:84
  186.1 7.3 %collective-permute-start.9 = (bf16[256,2048]{1,0:T(8,128)(2,1)S(1)}, bf16[256,2048]{1,0:T(8,128)(2,1)S(1)}, u32[]{:S(2)}, u32[]{:S(2)}) collective-permute-start(bf16[256,2048]{1,0:T(8,128)(2,1)S(1)} %convolution_convert_fusion.2), channel_id=1, source_target_pairs={{0,1},{1,0},{2,3},{3,2},{4,5},{5,4},{6,7},{7,6},{8,9},{9,8},{10,11... | collective-permute-start | bytes 3145736 | tf_op jit(solution)/shard_map/ppermute | solution.py:84
  186.8 34.3 %collective-permute-start.57 = (bf16[256,1024]{1,0:T(8,128)(2,1)S(1)}, bf16[256,1024]{1,0:T(8,128)(2,1)S(1)}, u32[]{:S(2)}, u32[]{:S(2)}) collective-permute-start(bf16[256,1024]{1,0:T(8,128)(2,1)S(1)} %pad_maximum_fusion.22), channel_id=1, source_target_pairs={{0,1},{1,0},{2,3},{3,2},{4,5},{5,4},{6,7},{7,6},{8,9},{9,8},{10,11... | collective-permute-start | bytes 1572872 | tf_op jit(solution)/shard_map/ppermute | solution.py:81
  192.7 14.8 %collective-permute-start.22 = (bf16[128,2048]{1,0:T(8,128)(2,1)S(1)}, bf16[128,2048]{1,0:T(8,128)(2,1)S(1)}, u32[]{:S(2)}, u32[]{:S(2)}) collective-permute-start(bf16[128,2048]{1,0:T(8,128)(2,1)S(1)} %slice.838), channel_id=1, source_target_pairs={{0,2},{1,3},{2,0},{3,1},{4,6},{5,7},{6,4},{7,5},{8,10},{9,11},{10,... | collective-permute-start | bytes 1572872 | tf_op jit(solution)/shard_map/ppermute | solution.py:85
  199.4 19.0 %collective-permute-start.10 = (bf16[128,2048]{1,0:T(8,128)(2,1)S(1)}, bf16[128,2048]{1,0:T(8,128)(2,1)S(1)}, u32[]{:S(2)}, u32[]{:S(2)}) collective-permute-start(bf16[128,2048]{1,0:T(8,128)(2,1)S(1)} %slice.839), channel_id=1, source_target_pairs={{0,2},{1,3},{2,0},{3,1},{4,6},{5,7},{6,4},{7,5},{8,10},{9,11},{10,... | collective-permute-start | bytes 1572872 | tf_op jit(solution)/shard_map/ppermute | solution.py:85
  221.1 95.3 %collective-permute-start.58 = (bf16[512,2048]{1,0:T(8,128)(2,1)S(1)}, bf16[512,2048]{1,0:T(8,128)(2,1)S(1)}, u32[]{:S(2)}, u32[]{:S(2)}) collective-permute-start(bf16[512,2048]{1,0:T(8,128)(2,1)S(1)} %get-tuple-element.146), channel_id=1, source_target_pairs={{0,16},{16,0},{1,17},{17,1},{2,18},{18,2},{3,19},{19,3},{4,20},{20... | collective-permute-start | bytes 6291464 | tf_op jit(solution)/shard_map/ppermute | solution.py:138
  221.7 101.9 %collective-permute-start.66 = (bf16[512,2048]{1,0:T(8,128)(2,1)S(1)}, bf16[512,2048]{1,0:T(8,128)(2,1)S(1)}, u32[]{:S(2)}, u32[]{:S(2)}) collective-permute-start(bf16[512,2048]{1,0:T(8,128)(2,1)S(1)} %get-tuple-element.44), channel_id=1, source_target_pairs={{0,16},{16,0},{1,17},{17,1},{2,18},{18,2},{3,19},{19,3},{4,20},{20... | collective-permute-start | bytes 6291464 | tf_op jit(solution)/shard_map/ppermute | solution.py:138
  228.1 6.3 %collective-permute-start.11 = (bf16[32,2048]{1,0:T(8,128)(2,1)S(1)}, bf16[32,2048]{1,0:T(8,128)(2,1)S(1)}, u32[]{:S(2)}, u32[]{:S(2)}) collective-permute-start(bf16[32,2048]{1,0:T(8,128)(2,1)S(1)} %get-tuple-element.107), channel_id=1, source_target_pairs={{0,12},{4,0},{8,4},{12,8},{1,13},{5,1},{9,5},{13,9},{2,14},{6,2},{... | collective-permute-start | bytes 393224 | tf_op jit(solution)/shard_map/ppermute | solution.py:91
  230.4 12.1 %collective-permute-start.12 = (bf16[32,2048]{1,0:T(8,128)(2,1)S(1)}, bf16[32,2048]{1,0:T(8,128)(2,1)S(1)}, u32[]{:S(2)}, u32[]{:S(2)}) collective-permute-start(bf16[32,2048]{1,0:T(8,128)(2,1)S(1)} %get-tuple-element.106), channel_id=1, source_target_pairs={{0,8},{4,12},{8,0},{12,4},{1,9},{5,13},{9,1},{13,5},{2,10},{6,14},... | collective-permute-start | bytes 393224 | tf_op jit(solution)/shard_map/ppermute | solution.py:91
  231.6 11.0 %collective-permute-start.13 = (bf16[32,2048]{1,0:T(8,128)(2,1)S(1)}, bf16[32,2048]{1,0:T(8,128)(2,1)S(1)}, u32[]{:S(2)}, u32[]{:S(2)}) collective-permute-start(bf16[32,2048]{1,0:T(8,128)(2,1)S(1)} %get-tuple-element.105), channel_id=1, source_target_pairs={{0,4},{4,8},{8,12},{12,0},{1,5},{5,9},{9,13},{13,1},{2,6},{6,10},{... | collective-permute-start | bytes 393224 | tf_op jit(solution)/shard_map/ppermute | solution.py:91
  234.4 81.9 %collective-permute-start.23 = (bf16[128,2048]{1,0:T(8,128)(2,1)S(1)}, bf16[128,2048]{1,0:T(8,128)(2,1)S(1)}, u32[]{:S(2)}, u32[]{:S(2)}) collective-permute-start(bf16[128,2048]{1,0:T(8,128)(2,1)S(1)} %get-tuple-element.42), channel_id=1, source_target_pairs={{0,2},{1,3},{2,0},{3,1},{4,6},{5,7},{6,4},{7,5},{8,10},{9,11},{10,... | collective-permute-start | bytes 1572872 | tf_op jit(solution)/shard_map/ppermute | solution.py:80
  242.6 95.6 %collective-permute-start.14 = (bf16[128,2048]{1,0:T(8,128)(2,1)S(1)}, bf16[128,2048]{1,0:T(8,128)(2,1)S(1)}, u32[]{:S(2)}, u32[]{:S(2)}) collective-permute-start(bf16[128,2048]{1,0:T(8,128)(2,1)S(1)} %pad_maximum_fusion.16), channel_id=1, source_target_pairs={{0,2},{1,3},{2,0},{3,1},{4,6},{5,7},{6,4},{7,5},{8,10},{9,11},{10,... | collective-permute-start | bytes 1572872 | tf_op jit(solution)/shard_map/ppermute | solution.py:80
  247.5 67.6 %collective-permute-start.54 = (f32[10240]{0:T(1024)S(1)}, f32[10240]{0:T(1024)S(1)}, u32[]{:S(2)}, u32[]{:S(2)}) collective-permute-start(f32[10240]{0:T(1024)S(1)} %add.813), channel_id=1, source_target_pairs={{0,16},{16,0},{1,17},{17,1},{2,18},{18,2},{3,19},{19,3},{4,20},{20... | collective-permute-start | bytes 122888 | tf_op jit(solution)/shard_map/ppermute | solution.py:252
  316.4 52.1 %collective-permute-start.24 = (bf16[256,2048]{1,0:T(8,128)(2,1)S(1)}, bf16[256,2048]{1,0:T(8,128)(2,1)S(1)}, u32[]{:S(2)}, u32[]{:S(2)}) collective-permute-start(bf16[256,2048]{1,0:T(8,128)(2,1)S(1)} %pad_maximum_fusion.8), channel_id=1, source_target_pairs={{0,1},{1,0},{2,3},{3,2},{4,5},{5,4},{6,7},{7,6},{8,9},{9,8},{10,11... | collective-permute-start | bytes 3145736 | tf_op jit(solution)/shard_map/ppermute | solution.py:81
  318.1 21.2 %collective-permute-start.61 = (bf16[256,1024]{1,0:T(8,128)(2,1)S(1)}, bf16[256,1024]{1,0:T(8,128)(2,1)S(1)}, u32[]{:S(2)}, u32[]{:S(2)}) collective-permute-start(bf16[256,1024]{1,0:T(8,128)(2,1)S(1)} %get-tuple-element.67), channel_id=1, source_target_pairs={{0,12},{4,0},{8,4},{12,8},{1,13},{5,1},{9,5},{13,9},{2,14},{6,2},{... | collective-permute-start | bytes 1572872 | tf_op jit(solution)/shard_map/ppermute | solution.py:126
  321.6 23.2 %collective-permute-start.59 = (bf16[256,1024]{1,0:T(8,128)(2,1)S(1)}, bf16[256,1024]{1,0:T(8,128)(2,1)S(1)}, u32[]{:S(2)}, u32[]{:S(2)}) collective-permute-start(bf16[256,1024]{1,0:T(8,128)(2,1)S(1)} %get-tuple-element.66), channel_id=1, source_target_pairs={{0,4},{4,8},{8,12},{12,0},{1,5},{5,9},{9,13},{13,1},{2,6},{6,10},{... | collective-permute-start | bytes 1572872 | tf_op jit(solution)/shard_map/ppermute | solution.py:125
  328.6 27.3 %collective-permute-start.69 = (bf16[256,1024]{1,0:T(8,128)(2,1)S(1)}, bf16[256,1024]{1,0:T(8,128)(2,1)S(1)}, u32[]{:S(2)}, u32[]{:S(2)}) collective-permute-start(bf16[256,1024]{1,0:T(8,128)(2,1)S(1)} %get-tuple-element.65), channel_id=1, source_target_pairs={{0,12},{4,0},{8,4},{12,8},{1,13},{5,1},{9,5},{13,9},{2,14},{6,2},{... | collective-permute-start | bytes 1572872 | tf_op jit(solution)/shard_map/ppermute | solution.py:126
  338.2 29.0 %collective-permute-start.67 = (bf16[256,1024]{1,0:T(8,128)(2,1)S(1)}, bf16[256,1024]{1,0:T(8,128)(2,1)S(1)}, u32[]{:S(2)}, u32[]{:S(2)}) collective-permute-start(bf16[256,1024]{1,0:T(8,128)(2,1)S(1)} %get-tuple-element.64), channel_id=1, source_target_pairs={{0,4},{4,8},{8,12},{12,0},{1,5},{5,9},{9,13},{13,1},{2,6},{6,10},{... | collective-permute-start | bytes 1572872 | tf_op jit(solution)/shard_map/ppermute | solution.py:125
  339.3 67.0 %collective-permute-start.15 = (bf16[256,2048]{1,0:T(8,128)(2,1)}, bf16[256,2048]{1,0:T(8,128)(2,1)}, u32[]{:S(2)}, u32[]{:S(2)}) collective-permute-start(bf16[256,2048]{1,0:T(8,128)(2,1)} %get-tuple-element.101), channel_id=1, source_target_pairs={{0,1},{1,0},{2,3},{3,2},{4,5},{5,4},{6,7},{7,6},{8,9},{9,8},{10,11... | collective-permute-start | bytes 3145736 | tf_op jit(solution)/shard_map/ppermute | solution.py:81
  344.7 79.0 %collective-permute-start.62 = (bf16[256,2048]{1,0:T(8,128)(2,1)}, bf16[256,2048]{1,0:T(8,128)(2,1)}, u32[]{:S(2)}, u32[]{:S(2)}) collective-permute-start(bf16[256,2048]{1,0:T(8,128)(2,1)} %pad_maximum_fusion.10), channel_id=1, source_target_pairs={{0,12},{4,0},{8,4},{12,8},{1,13},{5,1},{9,5},{13,9},{2,14},{6,2},{... | collective-permute-start | bytes 3145736 | tf_op jit(solution)/shard_map/ppermute | solution.py:132
  355.9 71.7 %collective-permute-start.60 = (bf16[256,2048]{1,0:T(8,128)(2,1)}, bf16[256,2048]{1,0:T(8,128)(2,1)}, u32[]{:S(2)}, u32[]{:S(2)}) collective-permute-start(bf16[256,2048]{1,0:T(8,128)(2,1)} %pad_maximum_fusion.9), channel_id=1, source_target_pairs={{0,4},{4,8},{8,12},{12,0},{1,5},{5,9},{9,13},{13,1},{2,6},{6,10},{... | collective-permute-start | bytes 3145736 | tf_op jit(solution)/shard_map/ppermute | solution.py:131
  400.2 46.7 %collective-permute-start.25 = (bf16[256,2048]{1,0:T(8,128)(2,1)S(1)}, bf16[256,2048]{1,0:T(8,128)(2,1)S(1)}, u32[]{:S(2)}, u32[]{:S(2)}) collective-permute-start(bf16[256,2048]{1,0:T(8,128)(2,1)S(1)} %fusion.18), channel_id=1, source_target_pairs={{0,1},{1,0},{2,3},{3,2},{4,5},{5,4},{6,7},{7,6},{8,9},{9,8},{10,11... | collective-permute-start | bytes 3145736 | tf_op jit(solution)/shard_map/ppermute | solution.py:84
  401.4 16.5 %collective-permute-start.47 = (bf16[512,256]{1,0:T(8,128)(2,1)S(1)}, bf16[512,256]{1,0:T(8,128)(2,1)S(1)}, u32[]{:S(2)}, u32[]{:S(2)}) collective-permute-start(bf16[512,256]{1,0:T(8,128)(2,1)S(1)} %get-tuple-element.82), channel_id=1, source_target_pairs={{0,12},{4,0},{8,4},{12,8},{1,13},{5,1},{9,5},{13,9},{2,14},{6,2},{... | collective-permute-start | bytes 786440 | tf_op jit(solution)/shard_map/ppermute | solution.py:126
  406.3 17.2 %collective-permute-start.45 = (bf16[512,256]{1,0:T(8,128)(2,1)S(1)}, bf16[512,256]{1,0:T(8,128)(2,1)S(1)}, u32[]{:S(2)}, u32[]{:S(2)}) collective-permute-start(bf16[512,256]{1,0:T(8,128)(2,1)S(1)} %get-tuple-element.81), channel_id=1, source_target_pairs={{0,4},{4,8},{8,12},{12,0},{1,5},{5,9},{9,13},{13,1},{2,6},{6,10},{... | collective-permute-start | bytes 786440 | tf_op jit(solution)/shard_map/ppermute | solution.py:125
  418.0 16.8 %collective-permute-start.48 = (bf16[512,512]{1,0:T(8,128)(2,1)S(1)}, bf16[512,512]{1,0:T(8,128)(2,1)S(1)}, u32[]{:S(2)}, u32[]{:S(2)}) collective-permute-start(bf16[512,512]{1,0:T(8,128)(2,1)S(1)} %pad_maximum_fusion.21), channel_id=1, source_target_pairs={{0,12},{4,0},{8,4},{12,8},{1,13},{5,1},{9,5},{13,9},{2,14},{6,2},{... | collective-permute-start | bytes 1572872 | tf_op jit(solution)/shard_map/ppermute | solution.py:132
  423.7 22.4 %collective-permute-start.46 = (bf16[512,512]{1,0:T(8,128)(2,1)S(1)}, bf16[512,512]{1,0:T(8,128)(2,1)S(1)}, u32[]{:S(2)}, u32[]{:S(2)}) collective-permute-start(bf16[512,512]{1,0:T(8,128)(2,1)S(1)} %pad_maximum_fusion.20), channel_id=1, source_target_pairs={{0,4},{4,8},{8,12},{12,0},{1,5},{5,9},{9,13},{13,1},{2,6},{6,10},{... | collective-permute-start | bytes 1572872 | tf_op jit(solution)/shard_map/ppermute | solution.py:131
  423.8 44.6 %collective-permute-start.70 = (bf16[256,2048]{1,0:T(8,128)(2,1)S(1)}, bf16[256,2048]{1,0:T(8,128)(2,1)S(1)}, u32[]{:S(2)}, u32[]{:S(2)}) collective-permute-start(bf16[256,2048]{1,0:T(8,128)(2,1)S(1)} %copy-done.45), channel_id=1, source_target_pairs={{0,12},{4,0},{8,4},{12,8},{1,13},{5,1},{9,5},{13,9},{2,14},{6,2},{... | collective-permute-start | bytes 3145736 | tf_op jit(solution)/shard_map/ppermute | solution.py:132
  427.6 62.9 %collective-permute-start.68 = (bf16[256,2048]{1,0:T(8,128)(2,1)S(1)}, bf16[256,2048]{1,0:T(8,128)(2,1)S(1)}, u32[]{:S(2)}, u32[]{:S(2)}) collective-permute-start(bf16[256,2048]{1,0:T(8,128)(2,1)S(1)} %copy-done.46), channel_id=1, source_target_pairs={{0,4},{4,8},{8,12},{12,0},{1,5},{5,9},{9,13},{13,1},{2,6},{6,10},{... | collective-permute-start | bytes 3145736 | tf_op jit(solution)/shard_map/ppermute | solution.py:131
  434.8 64.6 %collective-permute-start.35 = (bf16[512,1536]{0,1:T(8,128)(2,1)S(1)}, bf16[512,1536]{0,1:T(8,128)(2,1)S(1)}, u32[]{:S(2)}, u32[]{:S(2)}) collective-permute-start(bf16[512,1536]{0,1:T(8,128)(2,1)S(1)} %pad_maximum_fusion.4), channel_id=1, source_target_pairs={{0,16},{16,0},{1,17},{17,1},{2,18},{18,2},{3,19},{19,3},{4,20},{20... | collective-permute-start | bytes 4718600 | tf_op jit(solution)/shard_map/ppermute | solution.py:138
  446.3 47.5 %collective-permute-start.49 = (bf16[256,512]{1,0:T(8,128)(2,1)S(1)}, bf16[256,512]{1,0:T(8,128)(2,1)S(1)}, u32[]{:S(2)}, u32[]{:S(2)}) collective-permute-start(bf16[256,512]{1,0:T(8,128)(2,1)S(1)} %dynamic-slice_convert_fusion), channel_id=1, source_target_pairs={{0,16},{16,0},{1,17},{17,1},{2,18},{18,2},{3,19},{19,3},{4,20},{20... | collective-permute-start | bytes 786440 | tf_op jit(solution)/shard_map/ppermute | solution.py:138
  447.8 46.8 %collective-permute-start.26 = (bf16[128,2048]{1,0:T(8,128)(2,1)S(1)}, bf16[128,2048]{1,0:T(8,128)(2,1)S(1)}, u32[]{:S(2)}, u32[]{:S(2)}) collective-permute-start(bf16[128,2048]{1,0:T(8,128)(2,1)S(1)} %slice.837), channel_id=1, source_target_pairs={{0,2},{1,3},{2,0},{3,1},{4,6},{5,7},{6,4},{7,5},{8,10},{9,11},{10,... | collective-permute-start | bytes 1572872 | tf_op jit(solution)/shard_map/ppermute | solution.py:85
  496.6 29.3 %collective-permute-start.27 = (bf16[32,2048]{1,0:T(8,128)(2,1)S(1)}, bf16[32,2048]{1,0:T(8,128)(2,1)S(1)}, u32[]{:S(2)}, u32[]{:S(2)}) collective-permute-start(bf16[32,2048]{1,0:T(8,128)(2,1)S(1)} %get-tuple-element.93), channel_id=1, source_target_pairs={{0,12},{4,0},{8,4},{12,8},{1,13},{5,1},{9,5},{13,9},{2,14},{6,2},{... | collective-permute-start | bytes 393224 | tf_op jit(solution)/shard_map/ppermute | solution.py:91
  498.3 28.2 %collective-permute-start.28 = (bf16[32,2048]{1,0:T(8,128)(2,1)S(1)}, bf16[32,2048]{1,0:T(8,128)(2,1)S(1)}, u32[]{:S(2)}, u32[]{:S(2)}) collective-permute-start(bf16[32,2048]{1,0:T(8,128)(2,1)S(1)} %get-tuple-element.92), channel_id=1, source_target_pairs={{0,8},{4,12},{8,0},{12,4},{1,9},{5,13},{9,1},{13,5},{2,10},{6,14},... | collective-permute-start | bytes 393224 | tf_op jit(solution)/shard_map/ppermute | solution.py:91
  498.3 28.2 %collective-permute-start.29 = (bf16[32,2048]{1,0:T(8,128)(2,1)S(1)}, bf16[32,2048]{1,0:T(8,128)(2,1)S(1)}, u32[]{:S(2)}, u32[]{:S(2)}) collective-permute-start(bf16[32,2048]{1,0:T(8,128)(2,1)S(1)} %get-tuple-element.91), channel_id=1, source_target_pairs={{0,4},{4,8},{8,12},{12,0},{1,5},{5,9},{9,13},{13,1},{2,6},{6,10},{... | collective-permute-start | bytes 393224 | tf_op jit(solution)/shard_map/ppermute | solution.py:91
  499.4 6.4 %collective-permute-start.40 = (f32[4096]{0:T(1024)S(1)}, f32[4096]{0:T(1024)S(1)}, u32[]{:S(2)}, u32[]{:S(2)}) collective-permute-start(f32[4096]{0:T(1024)S(1)} %pad_maximum_fusion.30), channel_id=1, source_target_pairs={{0,1},{1,0},{2,3},{3,2},{4,5},{5,4},{6,7},{7,6},{8,9},{9,8},{10,11... | collective-permute-start | bytes 49160 | tf_op jit(solution)/shard_map/ppermute | solution.py:252
  506.6 23.4 %collective-permute-start.38 = (bf16[256,768]{1,0:T(8,128)(2,1)S(1)}, bf16[256,768]{1,0:T(8,128)(2,1)S(1)}, u32[]{:S(2)}, u32[]{:S(2)}) collective-permute-start(bf16[256,768]{1,0:T(8,128)(2,1)S(1)} %get-tuple-element.70), channel_id=1, source_target_pairs={{0,12},{4,0},{8,4},{12,8},{1,13},{5,1},{9,5},{13,9},{2,14},{6,2},{... | collective-permute-start | bytes 1179656 | tf_op jit(solution)/shard_map/ppermute | solution.py:126
  509.6 9.5 %collective-permute-start.42 = (f32[5120]{0:T(1024)S(1)}, f32[5120]{0:T(1024)S(1)}, u32[]{:S(2)}, u32[]{:S(2)}) collective-permute-start(f32[5120]{0:T(1024)S(1)} %pad_maximum_fusion.29), channel_id=1, source_target_pairs={{0,4},{4,0},{8,12},{12,8},{1,5},{5,1},{9,13},{13,9},{2,6},{6,2},{1... | collective-permute-start | bytes 61448 | tf_op jit(solution)/shard_map/ppermute | solution.py:252
  523.8 13.9 %collective-permute-start.36 = (bf16[256,768]{1,0:T(8,128)(2,1)S(1)}, bf16[256,768]{1,0:T(8,128)(2,1)S(1)}, u32[]{:S(2)}, u32[]{:S(2)}) collective-permute-start(bf16[256,768]{1,0:T(8,128)(2,1)S(1)} %get-tuple-element.69), channel_id=1, source_target_pairs={{0,4},{4,8},{8,12},{12,0},{1,5},{5,9},{9,13},{13,1},{2,6},{6,10},{... | collective-permute-start | bytes 1179656 | tf_op jit(solution)/shard_map/ppermute | solution.py:125
  525.9 16.9 %collective-permute-start.44 = (f32[5120]{0:T(1024)S(1)}, f32[5120]{0:T(1024)S(1)}, u32[]{:S(2)}, u32[]{:S(2)}) collective-permute-start(f32[5120]{0:T(1024)S(1)} %add.793), channel_id=1, source_target_pairs={{0,16},{16,0},{1,17},{17,1},{2,18},{18,2},{3,19},{19,3},{4,20},{20... | collective-permute-start | bytes 61448 | tf_op jit(solution)/shard_map/ppermute | solution.py:252
  526.5 12.5 %collective-permute-start.30 = (bf16[128,2048]{1,0:T(8,128)(2,1)S(1)}, bf16[128,2048]{1,0:T(8,128)(2,1)S(1)}, u32[]{:S(2)}, u32[]{:S(2)}) collective-permute-start(bf16[128,2048]{1,0:T(8,128)(2,1)S(1)} %pad_maximum_fusion.18), channel_id=1, source_target_pairs={{0,2},{1,3},{2,0},{3,1},{4,6},{5,7},{6,4},{7,5},{8,10},{9,11},{10,... | collective-permute-start | bytes 1572872 | tf_op jit(solution)/shard_map/ppermute | solution.py:80
  531.1 23.6 %collective-permute-start.39 = (bf16[256,1536]{1,0:T(8,128)(2,1)}, bf16[256,1536]{1,0:T(8,128)(2,1)}, u32[]{:S(2)}, u32[]{:S(2)}) collective-permute-start(bf16[256,1536]{1,0:T(8,128)(2,1)} %pad_maximum_fusion.14), channel_id=1, source_target_pairs={{0,12},{4,0},{8,4},{12,8},{1,13},{5,1},{9,5},{13,9},{2,14},{6,2},{... | collective-permute-start | bytes 2359304 | tf_op jit(solution)/shard_map/ppermute | solution.py:132
  538.8 30.9 %collective-permute-start.37 = (bf16[256,1536]{1,0:T(8,128)(2,1)}, bf16[256,1536]{1,0:T(8,128)(2,1)}, u32[]{:S(2)}, u32[]{:S(2)}) collective-permute-start(bf16[256,1536]{1,0:T(8,128)(2,1)} %pad_maximum_fusion.13), channel_id=1, source_target_pairs={{0,4},{4,8},{8,12},{12,0},{1,5},{5,9},{9,13},{13,1},{2,6},{6,10},{... | collective-permute-start | bytes 2359304 | tf_op jit(solution)/shard_map/ppermute | solution.py:131
  539.9 39.8 %collective-permute-start.31 = (bf16[256,2048]{1,0:T(8,128)(2,1)}, bf16[256,2048]{1,0:T(8,128)(2,1)}, u32[]{:S(2)}, u32[]{:S(2)}) collective-permute-start(bf16[256,2048]{1,0:T(8,128)(2,1)} %get-tuple-element.87), channel_id=1, source_target_pairs={{0,1},{1,0},{2,3},{3,2},{4,5},{5,4},{6,7},{7,6},{8,9},{9,8},{10,11... | collective-permute-start | bytes 3145736 | tf_op jit(solution)/shard_map/ppermute | solution.py:81
  (81 other events, 2202.6 us)

commit v2 on v1

v2 whole, which is shorter than its diff:
```python
import functools

import jax
import jax.numpy as jnp
from jax import lax
from jax.experimental import pallas as pl
from jax.experimental.pallas import tpu as pltpu
from jax.sharding import PartitionSpec as P

DH = 128
LOW = jnp.bfloat16
FULL = jnp.float32
TILE = 512


def flip(size, bit):
    return [(i, i ^ bit) for i in range(size)]


def shift(size, step):
    return [(i, (i + step) % size) for i in range(size)]


def after(value, *others):
    return lax.optimization_barrier((value, *others))[0]


class Order:
    def __init__(self):
        self.last = None

    def run(self, function, first, *others, needs=()):
        waits = list(needs) + ([] if self.last is None else [self.last])
        if waits:
            first = after(first, *waits)
        results = function(first, *others)
        self.last = results[-1] if isinstance(results, (list, tuple)) else results
        return results


def dot(left, right, dims):
    return lax.dot_general(left, right, (dims, ((), ())), preferred_element_type=FULL)


COLS = ((1,), (0,))
BOTH = ((1,), (1,))
ROWS = ((0,), (0,))


def shape_of(dims, kind):
    return jax.ShapeDtypeStruct(dims, kind)


def whole(dims):
    return pl.BlockSpec(dims, lambda *_: (0,) * len(dims))


def params(megabytes):
    return pltpu.CompilerParams(vmem_limit_bytes=megabytes << 20)


def cost(microseconds):
    flops = int(microseconds * 0.2 * 1153.5e6)
    return pl.CostEstimate(flops=flops, bytes_accessed=1, transcendentals=0)


def stack_rows(target, pieces):
    at = 0
    for piece in pieces:
        target[at : at + piece.shape[0], :] = piece[...]
        at += piece.shape[0]


def normalize(values):
    centered = values - jnp.mean(values, axis=-1, keepdims=True)
    variance = jnp.mean(centered * centered, axis=-1, keepdims=True)
    inverse = lax.rsqrt(variance + 1e-05)
    return centered * inverse, inverse


def norm_back(grad_norm, unit, inverse, gain):
    scaled = grad_norm * gain
    first = jnp.mean(scaled, axis=-1, keepdims=True)
    second = jnp.mean(scaled * unit, axis=-1, keepdims=True)
    return inverse * (scaled - first - unit * second)


def enter_kernel(count, gain, bias, *refs):
    pieces, (x_out, act_out) = refs[:count], refs[count:]
    stack_rows(x_out, pieces)
    unit, _ = normalize(x_out[...].astype(FULL))
    act_out[...] = (unit * gain[...].astype(FULL) + bias[...].astype(FULL)).astype(LOW)


def enter(gain, bias, pieces):
    rows, d_model = sum(p.shape[0] for p in pieces), pieces[0].shape[1]
    return pl.pallas_call(
        functools.partial(enter_kernel, len(pieces)),
        out_shape=[shape_of((rows, d_model), LOW)] * 2,
        compiler_params=params(16),
        cost_estimate=cost(2),
    )(gain, bias, *pieces)


def attention_kernel(scale, own, near, far, last, w_qkv, b_qkv, w_out, pos_row, pos_col, length, qkv_out, probs_out, mixed_out, keep_out, send_out, fold_out, act, bias, total):
    step = pl.program_id(0)
    half = act.shape[0] // 2

    @pl.when(step == 0)
    def _():
        stack_rows(act, (own, near, far, last))
        allowed = (pos_row[...] <= pos_col[...]) & (pos_row[...] < length[0])
        bias[...] = jnp.where(allowed, 0.0, -1e30)
        total[...] = jnp.zeros_like(total)

    for t in range(3):
        qkv_out[t] = (dot(act[...], w_qkv[t], COLS) + b_qkv[t][None]).astype(LOW)
    for h in range(w_out.shape[1] // DH):
        at = slice(h * DH, (h + 1) * DH)
        scores = dot(qkv_out[0, :, at], qkv_out[1, :, at], BOTH) * scale + bias[...]
        expo = jnp.exp(scores - jnp.max(scores, axis=-1, keepdims=True))
        probs = expo * (1.0 / jnp.sum(expo, axis=-1, keepdims=True))
        probs_out[h] = probs
        mixed_out[:, at] = dot(probs.astype(LOW), qkv_out[2, :, at], COLS).astype(LOW)
    total[...] += dot(mixed_out[...], w_out[...], BOTH)

    @pl.when(step == pl.num_programs(0) - 1)
    def _():
        keep_out[...] = total[:half]
        send_out[...] = total[half : half + half // 2].astype(LOW)
        fold_out[...] = total[half + half // 2 :].astype(LOW)


def attention(own, near, far, last, w_qkv, b_qkv, w_out, pos, length, group=2):
    d_model, width = w_out.shape
    rows = 4 * own.shape[0]
    cols = group * DH
    heads = width // DH
    return pl.pallas_call(
        functools.partial(attention_kernel, DH**-0.5),
        grid=(width // cols,),
        in_specs=[
            *[whole(own.shape)] * 4,
            pl.BlockSpec((3, d_model, cols), lambda i: (0, 0, i)),
            pl.BlockSpec((3, cols), lambda i: (0, i)),
            pl.BlockSpec((d_model, cols), lambda i: (0, i)),
            whole((1, rows)),
            whole((rows, 1)),
            pl.BlockSpec(memory_space=pltpu.SMEM),
        ],
        out_specs=[
            pl.BlockSpec((3, rows, cols), lambda i: (0, 0, i)),
            pl.BlockSpec((group, rows, rows), lambda i: (i, 0, 0)),
            pl.BlockSpec((rows, cols), lambda i: (0, i)),
            whole((rows // 2, d_model)),
            whole((rows // 4, d_model)),
            whole((rows // 4, d_model)),
        ],
        out_shape=[
            shape_of((3, rows, width), LOW),
            shape_of((heads, rows, rows), FULL),
            shape_of((rows, width), LOW),
            shape_of((rows // 2, d_model), FULL),
            shape_of((rows // 4, d_model), LOW),
            shape_of((rows // 4, d_model), LOW),
        ],
        scratch_shapes=[
            pltpu.VMEM((rows, d_model), LOW),
            pltpu.VMEM((rows, rows), FULL),
            pltpu.VMEM((rows, d_model), FULL),
        ],
        compiler_params=params(48),
        cost_estimate=cost(14),
    )(own, near, far, last, w_qkv, b_qkv, w_out, pos[None, :], pos[:, None], length)


def fold_kernel(got, keep, out):
    out[...] = (keep[...] + got[...].astype(FULL)).astype(LOW)


def fold(got, keep):
    rows, d_model = got.shape
    lower = pl.BlockSpec((rows, d_model), lambda i: (1, 0))
    return pl.pallas_call(
        fold_kernel,
        grid=(1,),
        in_specs=[whole(got.shape), lower],
        out_specs=whole((rows, d_model)),
        out_shape=shape_of((rows, d_model), LOW),
        compiler_params=params(16),
        cost_estimate=cost(1),
    )(got, keep)


def output_kernel(last, keep, got, resid, biases, out):
    down = keep[...] + got[...].astype(FULL) + last[...].astype(FULL)
    out[...] = (resid[...] + down + biases[1:].astype(FULL)).astype(LOW)


def output_of(last, keep, got, resid, biases):
    dims = resid.shape
    return pl.pallas_call(
        output_kernel,
        grid=(1,),
        in_specs=[whole(dims)] * 4 + [whole(biases.shape)],
        out_specs=whole(dims),
        out_shape=shape_of(dims, LOW),
        compiler_params=params(16),
        cost_estimate=cost(1.5),
    )(last, keep, got, resid, biases)


def middle_kernel(x_own, keep, got, last, biases, gain, bias, resid_out, act_out):
    attn = keep[...] + got[...].astype(FULL) + last[...].astype(FULL) + biases[:1].astype(FULL)
    resid = x_own[...].astype(FULL) + attn
    resid_out[...] = resid
    unit, _ = normalize(resid)
    act_out[...] = (unit * gain[...].astype(FULL) + bias[...].astype(FULL)).astype(LOW)


def middle(x_own, keep, got, last, biases, gain, bias):
    dims = x_own.shape
    return pl.pallas_call(
        middle_kernel,
        grid=(1,),
        in_specs=[whole(dims)] * 4 + [whole(biases.shape), whole(gain.shape), whole(bias.shape)],
        out_specs=[whole(dims)] * 2,
        out_shape=[shape_of(dims, FULL), shape_of(dims, LOW)],
        compiler_params=params(24),
        cost_estimate=cost(2),
    )(x_own, keep, got, last, biases, gain, bias)


def feed_kernel(own, near, far, last, dy_own, dy_near, dy_far, dy_last, w_up, b_up, w_down, gel_out, dup_out, sum_out, keep_out, send_out, fold_out, act, dy, total):
    step = pl.program_id(0)
    half = act.shape[0] // 2

    @pl.when(step == 0)
    def _():
        stack_rows(act, (own, near, far, last))
        stack_rows(dy, (dy_own, dy_near, dy_far, dy_last))
        total[...] = jnp.zeros_like(total)

    upper = dot(act[...], w_up[...], COLS) + b_up[...].astype(FULL)
    dgel = dot(dy[...], w_down[...], COLS)
    phi = 0.5 + 0.5 * lax.erf(upper * (0.5**0.5))
    gel_out[0] = (upper * phi).astype(LOW)
    slope = phi + upper * jnp.exp(-0.5 * upper * upper) * 0.3989422804014327
    dup = (dgel * slope).astype(LOW)
    dup_out[0] = dup
    sum_out[...] = jnp.sum(dup.astype(FULL), axis=0, keepdims=True)
    total[...] += dot(dup, w_up[...], BOTH)

    @pl.when(step == pl.num_programs(0) - 1)
    def _():
        keep_out[...] = total[:half]
        send_out[...] = total[half : half + half // 2].astype(LOW)
        fold_out[...] = total[half + half // 2 :].astype(LOW)


def feed(own, near, far, last, dy, w_up, b_up, w_down):
    d_model, units = w_up.shape
    rows = 4 * own.shape[0]
    steps = units // TILE
    return pl.pallas_call(
        feed_kernel,
        grid=(steps,),
        in_specs=[
            *[whole(own.shape)] * 8,
            pl.BlockSpec((d_model, TILE), lambda i: (0, i)),
            pl.BlockSpec((1, TILE), lambda i: (0, i)),
            pl.BlockSpec((d_model, TILE), lambda i: (0, i)),
        ],
        out_specs=[
            pl.BlockSpec((1, rows, TILE), lambda i: (i, 0, 0)),
            pl.BlockSpec((1, rows, TILE), lambda i: (i, 0, 0)),
            pl.BlockSpec((1, TILE), lambda i: (0, i)),
            whole((rows // 2, d_model)),
            whole((rows // 4, d_model)),
            whole((rows // 4, d_model)),
        ],
        out_shape=[
            shape_of((steps, rows, TILE), LOW),
            shape_of((steps, rows, TILE), LOW),
            shape_of((1, units), FULL),
            shape_of((rows // 2, d_model), FULL),
            shape_of((rows // 4, d_model), LOW),
            shape_of((rows // 4, d_model), LOW),
        ],
        scratch_shapes=[
            pltpu.VMEM((rows, d_model), LOW),
            pltpu.VMEM((rows, d_model), LOW),
            pltpu.VMEM((rows, d_model), FULL),
        ],
        compiler_params=params(48),
        cost_estimate=cost(20),
    )(own, near, far, last, *dy, w_up, b_up, w_down)


def gel_kernel(own, near, far, last, w_up, b_up, gel_out, act):
    @pl.when(pl.program_id(0) == 0)
    def _():
        stack_rows(act, (own, near, far, last))

    upper = dot(act[...], w_up[...], COLS) + b_up[...].astype(FULL)
    gel_out[0] = (upper * (0.5 + 0.5 * lax.erf(upper * (0.5**0.5)))).astype(LOW)


def gel_first(own, near, far, last, w_up, b_up, steps):
    d_model = own.shape[1]
    rows = 4 * own.shape[0]
    return pl.pallas_call(
        gel_kernel,
        grid=(steps,),
        in_specs=[
            *[whole(own.shape)] * 4,
            pl.BlockSpec((d_model, TILE), lambda i: (0, i)),
            pl.BlockSpec((1, TILE), lambda i: (0, i)),
        ],
        out_specs=pl.BlockSpec((1, rows, TILE), lambda i: (i, 0, 0)),
        out_shape=shape_of((steps, rows, TILE), LOW),
        scratch_shapes=[pltpu.VMEM((rows, d_model), LOW)],
        compiler_params=params(32),
        cost_estimate=cost(2 * steps),
    )(own, near, far, last, w_up, b_up)


def down_kernel(gel, w_down, keep_out, send_out, fold_out, total):
    step = pl.program_id(0)
    half = total.shape[0] // 2
    part = dot(gel[0], w_down[...], BOTH)

    @pl.when(step == 0)
    def _():
        total[...] = part

    @pl.when(step > 0)
    def _():
        total[...] += part

    @pl.when(step == pl.num_programs(0) - 1)
    def _():
        keep_out[...] = total[:half]
        send_out[...] = total[half : half + half // 2].astype(LOW)
        fold_out[...] = total[half + half // 2 :].astype(LOW)


def down_part(gel, w_down):
    d_model, units = w_down.shape
    rows = gel.shape[1]
    return pl.pallas_call(
        down_kernel,
        grid=(units // TILE,),
        in_specs=[
            pl.BlockSpec((1, rows, TILE), lambda i: (i, 0, 0)),
            pl.BlockSpec((d_model, TILE), lambda i: (0, i)),
        ],
        out_specs=[whole((rows // 2, d_model))] + [whole((rows // 4, d_model))] * 2,
        out_shape=[shape_of((rows // 2, d_model), FULL)] + [shape_of((rows // 4, d_model), LOW)] * 2,
        scratch_shapes=[pltpu.VMEM((rows, d_model), FULL)],
        compiler_params=params(40),
        cost_estimate=cost(7),
    )(gel, w_down)


def turn_kernel(keep, got, last, resid, dy, gain, dh_out, dattn_out, sum_out):
    da2 = keep[...] + got[...].astype(FULL) + last[...].astype(FULL)
    unit, inverse = normalize(resid[...])
    dy_full = dy[...].astype(FULL)
    dh = dy_full + norm_back(da2, unit, inverse, gain[...].astype(FULL))
    dh_out[...] = dh
    dattn = dh.astype(LOW)
    dattn_out[...] = dattn
    sum_out[0:1] = jnp.sum(da2 * unit, axis=0, keepdims=True)
    sum_out[1:2] = jnp.sum(da2, axis=0, keepdims=True)
    sum_out[2:3] = jnp.sum(dattn.astype(FULL), axis=0, keepdims=True)
    sum_out[3:4] = jnp.sum(dy_full, axis=0, keepdims=True)


def turn(keep, got, last, resid, dy, gain):
    dims = resid.shape
    return pl.pallas_call(
        turn_kernel,
        grid=(1,),
        in_specs=[whole(dims)] * 5 + [whole(gain.shape)],
        out_specs=[whole(dims), whole(dims), whole((4, dims[1]))],
        out_shape=[shape_of(dims, FULL), shape_of(dims, LOW), shape_of((4, dims[1]), FULL)],
        compiler_params=params(24),
        cost_estimate=cost(3),
    )(keep, got, last, resid, dy, gain)


def back_kernel(scale, own, near, far, last, w_out, qkv, probs_in, w_qkv, dqkv_out, sum_out, keep_out, send_out, fold_out, act, total):
    step = pl.program_id(0)
    half = act.shape[0] // 2

    @pl.when(step == 0)
    def _():
        stack_rows(act, (own, near, far, last))
        total[...] = jnp.zeros_like(total)

    dmixed = dot(act[...], w_out[...], COLS).astype(LOW)
    for h in range(w_out.shape[1] // DH):
        at = slice(h * DH, (h + 1) * DH)
        probs = probs_in[h]
        dm = dmixed[:, at]
        dqkv_out[2, :, at] = dot(probs.astype(LOW), dm, ROWS).astype(LOW)
        dprobs = dot(dm, qkv[2, :, at], BOTH)
        terms = jnp.sum(probs * dprobs, axis=-1, keepdims=True)
        ds = (probs * (dprobs - terms) * scale).astype(LOW)
        dqkv_out[0, :, at] = dot(ds, qkv[1, :, at], COLS).astype(LOW)
        dqkv_out[1, :, at] = dot(ds, qkv[0, :, at], ROWS).astype(LOW)
    part = dot(dqkv_out[0], w_qkv[0], BOTH)
    part += dot(dqkv_out[1], w_qkv[1], BOTH)
    part += dot(dqkv_out[2], w_qkv[2], BOTH)
    total[...] += part
    for row, t in enumerate((0, 2)):
        sum_out[row : row + 1] = jnp.sum(dqkv_out[t].astype(FULL), axis=0, keepdims=True)

    @pl.when(step == pl.num_programs(0) - 1)
    def _():
        keep_out[...] = total[:half]
        send_out[...] = total[half : half + half // 2].astype(LOW)
        fold_out[...] = total[half + half // 2 :].astype(LOW)


def attention_back(own, near, far, last, w_out, qkv, probs, w_qkv, group=2):
    d_model, width = w_out.shape
    rows = qkv.shape[1]
    cols = group * DH
    return pl.pallas_call(
        functools.partial(back_kernel, DH**-0.5),
        grid=(width // cols,),
        in_specs=[
            *[whole(own.shape)] * 4,
            pl.BlockSpec((d_model, cols), lambda i: (0, i)),
            pl.BlockSpec((3, rows, cols), lambda i: (0, 0, i)),
            pl.BlockSpec((group, rows, rows), lambda i: (i, 0, 0)),
            pl.BlockSpec((3, d_model, cols), lambda i: (0, 0, i)),
        ],
        out_specs=[
            pl.BlockSpec((3, rows, cols), lambda i: (0, 0, i)),
            pl.BlockSpec((2, cols), lambda i: (0, i)),
            whole((rows // 2, d_model)),
            whole((rows // 4, d_model)),
            whole((rows // 4, d_model)),
        ],
        out_shape=[
            shape_of((3, rows, width), LOW),
            shape_of((2, width), FULL),
            shape_of((rows // 2, d_model), FULL),
            shape_of((rows // 4, d_model), LOW),
            shape_of((rows // 4, d_model), LOW),
        ],
        scratch_shapes=[pltpu.VMEM((rows, d_model), LOW), pltpu.VMEM((rows, d_model), FULL)],
        compiler_params=params(48),
        cost_estimate=cost(15),
    )(own, near, far, last, w_out, qkv, probs, w_qkv)


def leave_kernel(keep, got, last, x_own, dh, gain, grad_out, sum_out):
    da1 = keep[...] + got[...].astype(FULL) + last[...].astype(FULL)
    unit, inverse = normalize(x_own[...].astype(FULL))
    grad_out[...] = (dh[...] + norm_back(da1, unit, inverse, gain[...].astype(FULL))).astype(LOW)
    sum_out[0:1] = jnp.sum(da1 * unit, axis=0, keepdims=True)
    sum_out[1:2] = jnp.sum(da1, axis=0, keepdims=True)


def leave(keep, got, last, x_own, dh, gain):
    dims = x_own.shape
    return pl.pallas_call(
        leave_kernel,
        grid=(1,),
        in_specs=[whole(dims)] * 5 + [whole(gain.shape)],
        out_specs=[whole(dims), whole((2, dims[1]))],
        out_shape=[shape_of(dims, LOW), shape_of((2, dims[1]), FULL)],
        compiler_params=params(24),
        cost_estimate=cost(2.5),
    )(keep, got, last, x_own, dh, gain)


def place_kernel(items, mp, sub, spot, own, near, far, last, out):
    for at, source in enumerate((own, near, far, last)):
        for s in range(items):
            rows = slice(s * sub, (s + 1) * sub)
            out[spot[s], spot[items + at]] = source[rows, :].astype(out.dtype)


def place(own, near, far, last, spot, items, mp, kind):
    rows, d_model = own.shape
    sub = rows // items
    return pl.pallas_call(
        functools.partial(place_kernel, items, mp, sub),
        in_specs=[pl.BlockSpec(memory_space=pltpu.SMEM)] + [pl.BlockSpec(memory_space=pltpu.VMEM)] * 4,
        out_specs=pl.BlockSpec(memory_space=pltpu.VMEM),
        out_shape=shape_of((items, mp, sub, d_model), kind),
        compiler_params=params(24),
        cost_estimate=cost(3),
    )(spot, own, near, far, last).reshape(items, mp * sub, d_model)


def product_kernel(shifts, n_units, spots, *refs):
    units = refs[len(refs) - n_units - 1 : -1]
    out = refs[-1]
    for at in range(shifts):
        columns = refs[at * n_units : (at + 1) * n_units]
        part = sum(dot(c[...], u[0], ROWS) for c, u in zip(columns, units))
        rows = part.shape[0]
        out[0, at * rows : (at + 1) * rows] = part.astype(LOW)


def add_kernel(n_units, spots, *refs):
    columns, units = refs[:n_units], refs[n_units : 2 * n_units]
    got, out = refs[2 * n_units :]
    part = sum(dot(c[...], u[0], ROWS) for c, u in zip(columns, units))
    out[0] = (part + got[0].astype(FULL)).astype(LOW)


def products(kernel, blocks, chunk, spots, columns, units, tiles, more=()):
    rows, first, steps = units[0].shape[1], tiles[0], len(tiles)
    in_specs, args = [], []
    for k in blocks:
        for array, base in columns:
            in_specs.append(pl.BlockSpec((rows, chunk), lambda i, spots, at=base + k: (0, spots[at])))
            args.append(array)
    for array in units:
        start = first if array.shape[0] != steps else 0
        in_specs.append(pl.BlockSpec((1, rows, TILE), lambda i, spots, start=start: (start + i, 0, 0)))
        args.append(array)
    for array, block in more:
        in_specs.append(pl.BlockSpec((1, chunk, TILE), lambda i, spots, block=block: (i, block, 0)))
        args.append(array)
    size = chunk * len(blocks)
    return pl.pallas_call(
        kernel,
        grid_spec=pltpu.PrefetchScalarGridSpec(
            num_scalar_prefetch=1,
            grid=(steps,),
            in_specs=in_specs,
            out_specs=pl.BlockSpec((1, size, TILE), lambda i, spots: (i, 0, 0)),
        ),
        out_shape=shape_of((steps, size, TILE), LOW),
        compiler_params=params(32),
        cost_estimate=cost(0.6 * steps * len(blocks)),
    )(spots, *args)


def pass_kernel(mine, got, out):
    out[...] = (mine[...].astype(FULL) + got[...].astype(FULL)).astype(LOW)


def pass_on(got, mine, chunk):
    steps = mine.shape[0]
    tail = pl.BlockSpec((1, chunk, TILE), lambda i, j: (i, 1 + j, 0))
    return pl.pallas_call(
        pass_kernel,
        grid=(steps, 2),
        in_specs=[tail, tail],
        out_specs=pl.BlockSpec((1, chunk, TILE), lambda i, j: (i, j, 0)),
        out_shape=shape_of((steps, 2 * chunk, TILE), LOW),
        compiler_params=params(16),
        cost_estimate=cost(steps),
    )(mine, got)


def finish_kernel(inner, mine, got, across, near, last, *refs):
    out = refs[-1]

    @pl.when(inner[0] == 1)
    def _():
        out[...] = (mine[...].astype(FULL) + got[...].astype(FULL) + across[...].astype(FULL)).reshape(out.shape)

    @pl.when(inner[0] == 0)
    def _():
        out[...] = (near[...].astype(FULL) + last[...].astype(FULL)).reshape(out.shape)


def finish(last, inner, mine, got, across, near, tiles, total, split, before):
    steps, chunk, _ = near.shape
    first = tiles[0]
    head = pl.BlockSpec((1, chunk, TILE), lambda i: (i, 0, 0))
    in_specs = [pl.BlockSpec(memory_space=pltpu.SMEM)] + [head] * 5
    args = [inner, mine, got, across, near, last]
    aliases = {}
    if before is not None:
        in_specs.append(pl.BlockSpec(memory_space=pl.ANY))
        args.append(before)
        aliases = {6: 0}
    if split:
        out_spec = pl.BlockSpec((1, chunk, TILE), lambda i: (first + i, 0, 0))
        out_shape = shape_of((total, chunk, TILE), FULL)
    else:
        out_spec = pl.BlockSpec((chunk, TILE), lambda i: (0, first + i))
        out_shape = shape_of((chunk, total * TILE), FULL)
    return pl.pallas_call(
        finish_kernel,
        grid=(steps,),
        in_specs=in_specs,
        out_specs=out_spec,
        out_shape=out_shape,
        input_output_aliases=aliases,
        compiler_params=params(16),
        cost_estimate=cost(steps),
    )(*args)


def on_device(
    dp,
    blk,
    mp,
    inputs,
    lengths,
    w_qkv,
    b_qv,
    w_out,
    out_biases,
    ln_gains,
    ln_shifts,
    w_up,
    b_up,
    w_down,
    cotangent,
):
    items, block_len, d_model = inputs.shape
    width = w_qkv.shape[2]
    sub = block_len // mp
    own_rows = blk * sub
    rows = own_rows * mp
    chunk = d_model // (dp * blk)
    half_cols = blk * chunk
    paired = dp == 2
    order = Order()
    x, z, me = lax.axis_index("dp"), lax.axis_index("blk"), lax.axis_index("mp")

    def to_items(array):
        mine = lax.dynamic_slice_in_dim(array, me * sub, sub, axis=1)
        parts = [lax.dynamic_index_in_dim(mine, z, 0, keepdims=False)]
        for s in range(1, blk):
            piece = lax.dynamic_index_in_dim(mine, lax.rem(z + s, blk), 0, keepdims=False)
            parts.append(lax.ppermute(piece, "blk", shift(blk, s)))
        return parts

    def swap_core(array):
        return lax.ppermute(array, "mp", flip(mp, 1))

    def swap_y(array):
        return lax.ppermute(array, "mp", flip(mp, 2))

    def swap_dp(array):
        return lax.ppermute(array, "dp", flip(dp, 1))

    def join(parts):
        return jnp.concatenate(parts, axis=0)

    def gather_mp(own):
        near = swap_y(own)
        return own, near, swap_core(own), swap_core(near)

    spot = jnp.stack(
        [lax.rem(z + s, blk) for s in range(blk)] + [me ^ j for j in (0, 2, 1, 3)]
    ).astype(jnp.int32)

    def from_items(own):
        parts = [own[:sub]]
        for s in range(1, blk):
            parts.append(lax.ppermute(own[s * sub : (s + 1) * sub], "blk", shift(blk, -s)))
        return join(parts)

    in_block = jnp.arange(sub, dtype=jnp.int32)
    block_of = lax.rem(z - jnp.arange(blk, dtype=jnp.int32) + blk, blk)

    def positions_of(q):
        return (block_of[:, None] * block_len + q * sub + in_block[None, :]).reshape(-1)

    pos = jnp.concatenate([positions_of(me ^ j) for j in (0, 2, 1, 3)])
    length = lax.dynamic_slice_in_dim(lengths, z, 1)

    def other_half(array):
        return lax.dynamic_slice_in_dim(array, (1 - x) * half_cols, half_cols, axis=1)

    line = [jnp.where(z < blk // 2, k, blk - 1 - k) for k in range(blk)]
    inner = jnp.where((z == 0) | (z == blk - 1), 0, 1).astype(jnp.int32)[None]
    spots = jnp.stack(
        [x * blk + at for at in line] + line + [blk + at for at in line]
    ).astype(jnp.int32)
    to_inner, across, to_end = [(0, 1), (3, 2)], [(1, 2), (2, 1)], [(1, 0), (2, 3)]

    class Piece:
        def __init__(self, columns, units, tiles):
            self.args = (chunk, spots, columns, units, tiles)
            self.tiles = tiles

        def start(self, needs=()):
            kernel = functools.partial(product_kernel, blk - 1, len(self.args[3]))
            self.mine = order.run(lambda first: products(kernel, (1, 2, 3), chunk, spots, [(first, self.args[2][0][1])] + self.args[2][1:], self.args[3], self.tiles), self.args[2][0][0], needs=needs)
            self.got = lax.ppermute(self.mine, "blk", to_inner)

        def cross(self, needs=()):
            send = order.run(pass_on, self.got, self.mine, chunk, needs=needs)
            self.across = lax.ppermute(send, "blk", across)

        def back(self):
            kernel = functools.partial(add_kernel, len(self.args[3]))
            self.near = order.run(lambda got: products(kernel, (0,), chunk, spots, self.args[2], self.args[3], self.tiles, [(got, 1)]), self.across)
            self.last = lax.ppermute(self.near, "blk", to_end)

        def end(self, total, split=False, before=None):
            return order.run(finish, self.last, inner, self.mine, self.got, self.across, self.near, self.tiles, total, split, before)

    def grad_plain(full, unit):
        part = jnp.einsum("rd,trc->dtc", full, unit, preferred_element_type=FULL).astype(LOW)
        part = lax.psum_scatter(part, ("dp", "blk"), scatter_dimension=0, tiled=True)
        return part.astype(FULL)

    w_three = w_qkv.transpose(1, 0, 2)
    b_three = jnp.stack([b_qv[0], jnp.zeros_like(b_qv[0]), b_qv[1]]).astype(FULL)
    gain_one, gain_two = ln_gains[:1], ln_gains[1:]
    shift_one, shift_two = ln_shifts[:1], ln_shifts[1:]

    def sum_over(array, axis, size):
        bit = 1
        while bit < size:
            array = array + lax.ppermute(array, axis, flip(size, bit))
            bit *= 2
        return array

    x_own, act_one_own = enter(gain_one, shift_one, to_items(inputs))
    order.last = act_one_own
    act_one_parts = gather_mp(act_one_own)
    valid = (pos[:own_rows] < length).astype(LOW)[:, None]
    dy_own = join(to_items(cotangent)) * valid
    dy_near = swap_y(after(dy_own, act_one_parts[1]))
    qkv, probs, mixed, keep, got, fold_got = order.run(
        attention, act_one_parts[0], *act_one_parts[1:], w_three, b_three, w_out, pos, length, needs=[dy_own]
    )
    got, fold_got = swap_core(got), swap_core(fold_got)
    if paired:
        halves_one = swap_dp(jnp.concatenate([other_half(act_one_own), other_half(dy_own)], axis=1))
        mixed_other = swap_dp(after(mixed, halves_one))
    last = swap_y(order.run(fold, fold_got, keep, needs=[dy_near]))
    dy_parts = dy_own, dy_near, swap_core(dy_own), swap_core(dy_near)
    resid, act_two_own = order.run(middle, x_own, keep, got, last, out_biases, gain_two, shift_two, needs=dy_parts)
    act_two_parts = gather_mp(act_two_own)
    tiles = w_up.shape[1] // TILE
    some = tiles // 2
    b_row = b_up[None]
    needs = []
    if paired:
        halves_near = swap_y(after(halves_one, act_two_parts[1]))
        needs = [mixed_other]
    gel_part = order.run(gel_first, act_two_parts[0], *act_two_parts[1:], w_up, b_row, some, needs=needs)
    if paired:
        gel_part_other = swap_dp(gel_part)
    gel, dup, up_sum, keep, got, fold_got = order.run(
        feed, act_two_parts[0], *act_two_parts[1:], dy_parts, w_up, b_row, w_down
    )
    got, fold_got = swap_core(got), swap_core(fold_got)
    dy = join(dy_parts)
    needs = []
    if paired:
        halves_one = join([halves_one, halves_near, swap_core(halves_one), swap_core(halves_near)])
        gel_rest_other = swap_dp(gel[some:])
        needs = [halves_one]
    last = swap_y(order.run(fold, fold_got, keep, needs=needs))
    da2 = keep, got, last
    if paired:
        columns = [(dy, 0), (halves_one, 2 * blk)]
        g0 = Piece(columns, [gel_part, gel_part_other], list(range(some)))
        g1 = Piece(columns, [gel, gel_rest_other], list(range(some, tiles)))
        g0.start()
    down_keep, down_got, down_fold = order.run(down_part, gel, w_down)
    down_got, down_fold = swap_core(down_got), swap_core(down_fold)
    dh, dattn_own, sums_two = order.run(turn, da2[0], *da2[1:], resid, dy_own, gain_two)
    dattn_parts = gather_mp(dattn_own)
    if paired:
        halves_two = swap_dp(
            after(
                jnp.concatenate([other_half(act_two_own), other_half(dattn_own)], axis=1),
                gel_rest_other,
            )
        )
        g1.start()
        dup_part_other = swap_dp(after(dup[:some], halves_two))
    down_near = order.run(fold, down_fold, down_keep)
    down_last = swap_y(after(down_near, dattn_parts[1]))
    needs = []
    if paired:
        halves_near = swap_y(after(halves_two, dattn_parts[1]))
        needs = [halves_two, g0.got]
    dqkv, qkv_sum, keep, got, fold_got = order.run(
        attention_back, dattn_parts[0], *dattn_parts[1:], w_out, qkv, probs, w_three, needs=needs
    )
    got, fold_got = swap_core(got), swap_core(fold_got)
    act_one, act_two, dattn = join(act_one_parts), join(act_two_parts), join(dattn_parts)
    needs = []
    if paired:
        halves_two = join([halves_two, halves_near, swap_core(halves_two), swap_core(halves_near)])
        columns = [(act_two, 0), (halves_two, blk)]
        u0 = Piece(columns, [dup, dup_part_other], list(range(some)))
        g0.cross()
        u0.start(needs=[halves_near])
        dup_rest_other = swap_dp(after(dup[some:], dup_part_other))
        u1 = Piece(columns, [dup, dup_rest_other], list(range(some, tiles)))
        dqkv_other = swap_dp(after(dqkv, dup_rest_other))
        needs = [g1.got]
    last = swap_y(order.run(fold, fold_got, keep))
    da1 = keep, got, last
    output = order.run(output_of, down_last, down_keep, down_got, resid, out_biases)
    output = from_items(output)
    input_grad, sums_one = order.run(leave, da1[0], *da1[1:], x_own, dh, gain_one, needs=needs)
    input_grad = from_items(input_grad)
    sums = jnp.concatenate([sums_one, sums_two], axis=0).reshape(-1)
    sums = sum_over(sums, "mp", mp)
    sums = jnp.concatenate([sums, qkv_sum.reshape(-1), up_sum.reshape(-1)])
    output = gather_mp(output)
    input_grad = gather_mp(input_grad)
    if paired:
        g1.cross()
        g0.back()
        u1.start()
        grad_down = g0.end(tiles)
    output = order.run(place, output[0], *output[1:], spot, items, mp, LOW)
    sums = sums + lax.ppermute(sums, "blk", flip(blk, 1))
    if paired:
        g1.back()
        columns = [(act_one, 0), (halves_one, blk)]
        q0 = Piece(columns, [dqkv, dqkv_other], [0, 1])
        q1 = Piece(columns, [dqkv, dqkv_other], [2])
        q0.start(needs=[u0.got, sums])
        u0.cross()
        grad_down = g1.end(tiles, before=grad_down)
    sums = sums + lax.ppermute(sums, "blk", flip(blk, 2))
    input_grad = order.run(place, input_grad[0], *input_grad[1:], spot, items, mp, FULL)
    if paired:
        q1.start()
        columns = [(dattn, 0), (halves_two, 2 * blk)]
        o0 = Piece(columns, [mixed[None], mixed_other[None]], [0])
        o0.start(needs=[u1.got, sums])
    sums = sum_over(sums, "dp", dp)
    if paired:
        u1.cross()
        u0.back()
        grad_up = u0.end(tiles)
        q0.cross(needs=[sums])
        u1.back()
        grad_up = u1.end(tiles, before=grad_up)
        q1.cross()
        q0.back()
        o0.cross()
        q1.back()
        grad_qkv = q0.end(3, True)
        o0.back()
        grad_qkv = q1.end(3, True, before=grad_qkv).transpose(1, 0, 2)
        grad_out = o0.end(1)
    else:
        grad_down = grad_plain(dy, gel).reshape(chunk, -1)
        grad_up = grad_plain(act_two, dup).reshape(chunk, -1)
        grad_out = grad_plain(dattn, mixed[None]).reshape(chunk, -1)
        grad_qkv = grad_plain(act_one, dqkv)

    per_token = sums[: 6 * d_model].reshape(6, d_model)
    grad_qv_bias = sums[6 * d_model : 6 * d_model + 2 * width].reshape(2, width)
    return (
        output,
        input_grad,
        grad_qkv,
        grad_qv_bias,
        grad_out,
        per_token[4:6],
        jnp.stack([per_token[0], per_token[2]]),
        jnp.stack([per_token[1], per_token[3]]),
        grad_up,
        sums[6 * d_model + 2 * width :],
        grad_down,
    )


def solution(mesh):
    sizes = [mesh.shape[name] for name in ("dp", "blk", "mp")]
    in_specs = (
        P("dp", "blk", None),
        P("dp"),
        P(None, None, "mp"),
        P(None, "mp"),
        P(None, "mp"),
        P(),
        P(),
        P(),
        P(None, "mp"),
        P("mp"),
        P(None, "mp"),
        P("dp", "blk", None),
    )
    out_specs = (
        P("dp", "blk", None),
        P("dp", "blk", None),
        P(("dp", "blk"), None, "mp"),
        P(None, "mp"),
        P(("dp", "blk"), "mp"),
        P(),
        P(),
        P(),
        P(("dp", "blk"), "mp"),
        P("mp"),
        P(("dp", "blk"), "mp"),
    )

    def step(*arrays):
        return on_device(*sizes, *arrays)

    return jax.shard_map(
        step, mesh=mesh, in_specs=in_specs, out_specs=out_specs, check_vma=False
    )
```

time: 595 us -> 489 us (0.82)
  matrix products: 148 us -> 0 us
  Pallas kernels: 0 us -> 134 us
  waiting for transfers between devices: 295 us -> 185 us
  starting transfers between devices: 68.2 us -> 101 us
  other arithmetic: 33.8 us -> 6.92 us
  local copies, waits for them, and re-layouts: 38.7 us -> 56.6 us
    dot_general x51 -> x0, matrix products: 142 us -> none  [the longest x46 120 us: dot(): lax.dot_general(left, right, (dims, ((), ())), preferred_element_type=FULL)]
    pallas_call x0 -> x44, Pallas kernels: none -> 134 us  [the longest x14 36.5 us: products(): pl.pallas_call(kernel, grid_spec=pltpu.PrefetchScalarGridSpec(num_scalar_...]
    ppermute x10 -> x3, waiting for transfers between devices: 77.7 us -> 3.51 us  [sum_over(): array = array + lax.ppermute(array, axis, flip(size, bit))]
    ppermute x42 -> x59, waiting for transfers between devices: 185 us -> 124 us  [the longest x12 44.7 us: swap_y(): return lax.ppermute(array, 'mp', flip(mp, 2))]
    ppermute x6, waiting for transfers between devices: 10.3 us -> 55.1 us  [from_items(): lax.ppermute(own[s * sub:(s + 1) * sub], 'blk', shift(blk, -s))]
    unnamed x166 -> x205, local copies, waits for them, and re-layouts: 15.6 us -> 40.2 us
    ppermute x42 -> x59, starting transfers between devices: 37.4 us -> 61.5 us  [the longest x7 26.3 us: start(): self.got = lax.ppermute(self.mine, 'blk', to_inner)]
    ppermute x6, waiting for transfers between devices: 15.4 us -> 0.02 us  [to_items(): parts.append(lax.ppermute(piece, 'blk', shift(blk, s)))]
  transfers between devices with their start and end apart: 71 -> 82, of which waited for: 33 -> 24; matrix products, arithmetic and copies ran while one was open for 32% -> 7% of each run, Pallas kernels for 0% -> 27%
where the time goes in v2:
time: 489 us; the launch traced here: 485 us
  waiting for transfers between devices  185 us (38%)
  Pallas kernels  134 us (27%)
  starting transfers between devices  101 us (21%)
  local copies, waits for them, and re-layouts  56.6 us (12%)
  other arithmetic  6.92 us (1%)
    ppermute x6, waiting for transfers between devices, from_items(): lax.ppermute(own[s * sub:(s + 1) * sub], 'blk', shift(blk, -s))  55.1 us
    ppermute x12, waiting for transfers between devices, swap_y(): return lax.ppermute(array, 'mp', flip(mp, 2))  44.7 us
    ppermute x7, waiting for transfers between devices, back(): self.last = lax.ppermute(self.near, 'blk', to_end)  44 us
    unnamed x205, local copies, waits for them, and re-layouts  40.2 us
    pallas_call x14, Pallas kernels, products(): pl.pallas_call(kernel, grid_spec=pltpu.PrefetchScalarGridSpec(num_scalar_...  36.5 us
    ppermute x1, waiting for transfers between devices, on_device(): sums = sums + lax.ppermute(sums, 'blk', flip(blk, 1))  27.6 us
    ppermute x7, starting transfers between devices, start(): self.got = lax.ppermute(self.mine, 'blk', to_inner)  26.3 us
    pallas_call x1, Pallas kernels, feed(): pl.pallas_call(feed_kernel, grid=(steps,), in_specs=[*[whole(own.shape)]...  19.4 us
  transfers between devices with their start and end apart: 82, of which 24 were waited for; matrix products, arithmetic and copies ran while one was open for 7% of the time, Pallas kernels for 27%

profile of v2, /device:TPU:0, one launch (start us, length us, event | category | flops | bytes accessed | tf_op | source)
XLA Modules:
  0.0 485.2 jit_solution(6170356072419298142)
XLA Ops:
  2.0 3.1 collective-permute-start
  5.1 2.6 collective-permute-start.1
  13.9 7.7 %collective-permute-start.3 = (bf16[32,2048]{1,0:T(8,128)(2,1)S(1)}, bf16[32,2048]{1,0:T(8,128)(2,1)S(1)}, u32[]{:S(2)}, u32[]{:S(2)}) collective-permute-start(bf16[32,2048]{1,0:T(8,128)(2,1)S(1)} %get-tuple-element.176), channel_id=1, source_target_pairs={{0,4},{4,8},{8,12},{12,0},{1,5},{5,9},{9,13},{13,1},{2,6},{6,10},{... | collective-permute-start | bytes 393224 | tf_op jit(solution)/shard_map/ppermute | solution.py:640
  25.2 6.8 %collective-permute-done.6.near = bf16[128,2048]{1,0:T(8,128)(2,1)S(1)} collective-permute-done((bf16[128,2048]{1,0:T(8,128)(2,1)S(1)}, bf16[128,2048]{1,0:T(8,128)(2,1)S(1)}, u32[]{:S(2)}, u32[]{:S(2)}) %collective-permute-start.6) | collective-permute-done | bytes 524320 | tf_op jit(solution)/shard_map/ppermute | solution.py:647
  42.1 14.9 %shard_map.204 = (bf16[3,512,512]{2,1,0:T(8,128)(2,1)S(1)}, f32[4,512,512]{2,1,0:T(8,128)}, bf16[512,512]{1,0:T(8,128)(2,1)}, f32[256,2048]{1,0:T(8,128)}, bf16[...) custom-call(bf16[128,2048]{1,0:T(8,128)(2,1)S(1)} %copy-done.68, bf16[128,2048]{1,0:T(8,128)(2,1)S(1)} %copy-done.78, ...), custom_call_target="tpu_custom_call" | custom-call | flops 3229799936 | bytes 1 | tf_op jit(solution)/shard_map/pallas_call | solution.py:139
  65.6 11.3 %collective-permute-done.14.last = bf16[128,2048]{1,0:T(8,128)(2,1)} collective-permute-done((bf16[128,2048]{1,0:T(8,128)(2,1)}, bf16[128,2048]{1,0:T(8,128)(2,1)}, u32[]{:S(2)}, u32[]{:S(2)}) %collective-permute-start.14) | collective-permute-done | bytes 524320 | tf_op jit(solution)/shard_map/ppermute | solution.py:647
  77.9 1.8 shard_map.206
  82.9 11.2 %collective-permute-done.17.near = bf16[128,2048]{1,0:T(8,128)(2,1)} collective-permute-done((bf16[128,2048]{1,0:T(8,128)(2,1)S(1)}, bf16[128,2048]{1,0:T(8,128)(2,1)}, u32[]{:S(2)}, u32[]{:S(2)}) %collective-permute-start.17) | collective-permute-done | bytes 524320 | tf_op jit(solution)/shard_map/ppermute | solution.py:647
  97.9 4.4 copy-done.11
  102.3 4.1 shard_map.207.refs_6_.refs_2_
  108.0 1.9 collective-permute-done.21
  109.9 19.4 %shard_map.208 = (bf16[4,512,512]{2,1,0:T(8,128)(2,1)}, bf16[4,512,512]{2,1,0:T(8,128)(2,1)}, f32[1,2048]{1,0:T(1,128)S(1)}, f32[256,2048]{1,0:T(8,128)}, bf16[1...) custom-call(bf16[128,2048]{1,0:T(8,128)(2,1)S(1)} %get-tuple-element.105.own, ...), custom_call_target="tpu_custom_call" | custom-call | flops 4614000128 | bytes 1 | tf_op jit(solution)/shard_map/pallas_call | solution.py:265
  130.0 2.4 slice.111
  137.4 3.0 shard_map.210.mine
  141.4 8.7 %collective-permute-start.32 = (bf16[2,768,512]{2,1,0:T(8,128)(2,1)S(1)}, bf16[2,768,512]{2,1,0:T(8,128)(2,1)}, u32[]{:S(2)}, u32[]{:S(2)}) collective-permute-start(bf16[2,768,512]{2,1,0:T(8,128)(2,1)S(1)} %shard_map.210.mine), channel_id=1, source_target_pairs={{0,4},{12,8},{1,5},{13,9},{2,6},{14,10},{3,7},{15,11},{16,20},{28,... | collective-permute-start | bytes 4718600 | tf_op jit(solution)/shard_map/ppermute | solution.py:696
  150.1 8.3 %shard_map.211 = (f32[256,2048]{1,0:T(8,128)S(1)}, bf16[128,2048]{1,0:T(8,128)(2,1)}, bf16[128,2048]{1,0:T(8,128)(2,1)S(1)}) custom-call(bf16[4,512,512]{2,1,0:T(8,128)(2,1)S(1)} %copy-done.12, bf16[2048,2048]{1,0:T(8,128)(2,1)S(1)} %bitcast.55), custom_call_target="tpu_custom_call" | custom-call | flops 1614899968 | bytes 1 | tf_op jit(solution)/shard_map/pallas_call | solution.py:351
  158.5 2.0 copy-done.42
  160.5 2.7 shard_map.212
  167.5 9.2 %collective-permute-done.29.near = bf16[128,2048]{1,0:T(8,128)(2,1)S(1)} collective-permute-done((bf16[128,2048]{1,0:T(8,128)(2,1)S(1)}, bf16[128,2048]{1,0:T(8,128)(2,1)S(1)}, u32[]{:S(2)}, u32[]{:S(2)}) %collective-permute-start.29) | collective-permute-done | bytes 524320 | tf_op jit(solution)/shard_map/ppermute | solution.py:647
  178.9 4.6 shard_map.213.mine
  183.5 2.4 collective-permute-start.45
  188.5 2.1 collective-permute-done.36
  195.2 15.6 %shard_map.215 = (bf16[3,512,512]{2,1,0:T(8,128)(2,1)S(1)}, f32[2,512]{1,0:T(2,128)S(1)}, f32[256,2048]{1,0:T(8,128)}, bf16[128,2048]{1,0:T(8,128)(2,1)}, bf16[128,2048]{1,0:T(8,128)(2,1)}) custom-call(bf16[128,2048]{1,0:T(8,128)(2,1)S(1)} %copy-done.45, bf16[128,2048]{1,0:T(8,128)(2,1)S(1)} %collective-permute-done.29.near, ...), custom_call_target="tpu_custom_call" | custom-call | flops 3460499968 | bytes 1 | tf_op jit(solution)/shard_map/pallas_call | solution.py:431
  213.9 3.7 shard_map.216
  217.6 1.7 collective-permute-start.44
  219.3 2.9 shard_map.217.mine
  223.1 2.2 collective-permute-done.30.last
  227.5 3.3 collective-permute-start.42
  230.8 3.6 collective-permute-done.43
  235.3 17.3 %collective-permute-done.42 = bf16[32,2048]{1,0:T(8,128)(2,1)S(1)} collective-permute-done((bf16[32,2048]{1,0:T(8,128)(2,1)S(1)}, bf16[32,2048]{1,0:T(8,128)(2,1)S(1)}, u32[]{:S(2)}, u32[]{:S(2)}) %collective-permute-start.42) | collective-permute-done | bytes 131104 | tf_op jit(solution)/shard_map/ppermute | solution.py:666
  255.3 1.8 pad_maximum_fusion.3.own
  260.7 2.2 shard_map.220
  263.0 3.0 shard_map.221
  267.0 3.2 shard_map.222.near
  272.9 3.5 collective-permute-start.55
  277.1 1.9 constant_dynamic-update-slice_fusion.15
  278.9 3.8 collective-permute-start.58
  283.5 2.3 collective-permute-start.54
  286.7 1.9 constant_dynamic-update-slice_fusion.14
  288.5 30.8 %collective-permute-done.54 = bf16[32,2048]{1,0:T(8,128)(2,1)S(1)} collective-permute-done((bf16[32,2048]{1,0:T(8,128)(2,1)S(1)}, bf16[32,2048]{1,0:T(8,128)(2,1)S(1)}, u32[]{:S(2)}, u32[]{:S(2)}) %collective-permute-start.54) | collective-permute-done | bytes 131104 | tf_op jit(solution)/shard_map/ppermute | solution.py:666
  320.6 1.9 constant_dynamic-update-slice_fusion.13.refs_0_.refs_2_.refs_4_
  322.5 2.2 collective-permute-done.53
  326.8 2.9 shard_map.223.mine
  329.7 2.4 shard_map.224.refs_0_
  332.1 4.5 collective-permute-start.67
  336.7 2.7 shard_map.225
  340.8 3.0 shard_map.226.near
  343.8 27.6 %collective-permute-done.61 = f32[15360]{0:T(1024)S(1)} collective-permute-done((f32[15360]{0:T(1024)S(1)}, f32[15360]{0:T(1024)S(1)}, u32[]{:S(2)}, u32[]{:S(2)}) %collective-permute-start.61) | collective-permute-done | bytes 61472 | tf_op jit(solution)/shard_map/ppermute | solution.py:823
  372.7 3.9 collective-permute-start.68
  376.6 2.9 shard_map.227.mine
  382.5 5.2 %collective-permute-done.57.last = bf16[2,256,512]{2,1,0:T(8,128)(2,1)S(1)} collective-permute-done((bf16[2,256,512]{2,1,0:T(8,128)(2,1)S(1)}, bf16[2,256,512]{2,1,0:T(8,128)(2,1)S(1)}, u32[]{:S(2)}, u32[]{:S(2)}) %collective-permute-start.57) | collective-permute-done | bytes 524320 | tf_op jit(solution)/shard_map/ppermute | solution.py:705
  387.9 2.1 shard_map.229
  390.0 2.8 shard_map.230
  394.4 3.0 shard_map.232.mine
  403.4 3.5 collective-permute-done.71
  406.9 12.7 %collective-permute-done.73.last = bf16[2,256,512]{2,1,0:T(8,128)(2,1)S(1)} collective-permute-done((bf16[2,256,512]{2,1,0:T(8,128)(2,1)S(1)}, bf16[2,256,512]{2,1,0:T(8,128)(2,1)S(1)}, u32[]{:S(2)}, u32[]{:S(2)}) %collective-permute-start.73) | collective-permute-done | bytes 524320 | tf_op jit(solution)/shard_map/ppermute | solution.py:705
  421.6 4.0 collective-permute-start.66
  429.9 12.1 %collective-permute-done.74.last = bf16[2,256,512]{2,1,0:T(8,128)(2,1)S(1)} collective-permute-done((bf16[2,256,512]{2,1,0:T(8,128)(2,1)S(1)}, bf16[2,256,512]{2,1,0:T(8,128)(2,1)S(1)}, u32[]{:S(2)}, u32[]{:S(2)}) %collective-permute-start.74) | collective-permute-done | bytes 524320 | tf_op jit(solution)/shard_map/ppermute | solution.py:705
  447.3 6.7 %collective-permute-done.76.got = bf16[1,768,512]{2,1,0:T(8,128)(2,1)S(1)} collective-permute-done((bf16[1,768,512]{2,1,0:T(8,128)(2,1)S(1)}, bf16[1,768,512]{2,1,0:T(8,128)(2,1)S(1)}, u32[]{:S(2)}, u32[]{:S(2)}) %collective-permute-start.76) | collective-permute-done | bytes 786464 | tf_op jit(solution)/shard_map/ppermute | solution.py:696
  459.2 5.3 %collective-permute-done.80.last = bf16[2,256,512]{2,1,0:T(8,128)(2,1)S(1)} collective-permute-done((bf16[2,256,512]{2,1,0:T(8,128)(2,1)S(1)}, bf16[2,256,512]{2,1,0:T(8,128)(2,1)S(1)}, u32[]{:S(2)}, u32[]{:S(2)}) %collective-permute-start.80) | collective-permute-done | bytes 524320 | tf_op jit(solution)/shard_map/ppermute | solution.py:705
  465.5 2.9 shard_map.244.near
  472.7 2.1 shard_map.245
  474.7 8.3 %collective-permute-done.81.last = bf16[1,256,512]{2,1,0:T(8,128)(2,1)} collective-permute-done((bf16[1,256,512]{2,1,0:T(8,128)(2,1)}, bf16[1,256,512]{2,1,0:T(8,128)(2,1)}, u32[]{:S(2)}, u32[]{:S(2)}) %collective-permute-start.81) | collective-permute-done | bytes 262176 | tf_op jit(solution)/shard_map/ppermute | solution.py:705
  483.0 1.9 shard_map.246
  (408 shorter events, 117.1 us)
Async XLA Ops:
  2.0 11.8 %collective-permute-start = (bf16[32,2048]{1,0:T(8,128)(2,1)S(1)}, bf16[32,2048]{1,0:T(8,128)(2,1)S(1)}, u32[]{:S(2)}, u32[]{:S(2)}) collective-permute-start(bf16[32,2048]{1,0:T(8,128)(2,1)S(1)} %get-tuple-element.180), channel_id=1, source_target_pairs={{0,4},{4,8},{8,12},{12,0},{1,5},{5,9},{9,13},{13,1},{2,6},{6,10},{... | collective-permute-start | bytes 393224 | tf_op jit(solution)/shard_map/ppermute | solution.py:640
  5.1 16.5 %collective-permute-start.1 = (bf16[32,2048]{1,0:T(8,128)(2,1)S(1)}, bf16[32,2048]{1,0:T(8,128)(2,1)S(1)}, u32[]{:S(2)}, u32[]{:S(2)}) collective-permute-start(bf16[32,2048]{1,0:T(8,128)(2,1)S(1)} %get-tuple-element.182), channel_id=1, source_target_pairs={{0,8},{4,12},{8,0},{12,4},{1,9},{5,13},{9,1},{13,5},{2,10},{6,14},... | collective-permute-start | bytes 393224 | tf_op jit(solution)/shard_map/ppermute | solution.py:640
  7.7 13.9 %collective-permute-start.2 = (bf16[32,2048]{1,0:T(8,128)(2,1)S(1)}, bf16[32,2048]{1,0:T(8,128)(2,1)S(1)}, u32[]{:S(2)}, u32[]{:S(2)}) collective-permute-start(bf16[32,2048]{1,0:T(8,128)(2,1)S(1)} %get-tuple-element.179), channel_id=1, source_target_pairs={{0,12},{4,0},{8,4},{12,8},{1,13},{5,1},{9,5},{13,9},{2,14},{6,2},{... | collective-permute-start | bytes 393224 | tf_op jit(solution)/shard_map/ppermute | solution.py:640
  10.3 21.9 %collective-permute-start.5 = (bf16[32,2048]{1,0:T(8,128)(2,1)S(1)}, bf16[32,2048]{1,0:T(8,128)(2,1)S(1)}, u32[]{:S(2)}, u32[]{:S(2)}) collective-permute-start(bf16[32,2048]{1,0:T(8,128)(2,1)S(1)} %get-tuple-element.177), channel_id=1, source_target_pairs={{0,12},{4,0},{8,4},{12,8},{1,13},{5,1},{9,5},{13,9},{2,14},{6,2},{... | collective-permute-start | bytes 393224 | tf_op jit(solution)/shard_map/ppermute | solution.py:640
  10.8 21.4 %collective-permute-start.4 = (bf16[32,2048]{1,0:T(8,128)(2,1)S(1)}, bf16[32,2048]{1,0:T(8,128)(2,1)S(1)}, u32[]{:S(2)}, u32[]{:S(2)}) collective-permute-start(bf16[32,2048]{1,0:T(8,128)(2,1)S(1)} %get-tuple-element.178), channel_id=1, source_target_pairs={{0,8},{4,12},{8,0},{12,4},{1,9},{5,13},{9,1},{13,5},{2,10},{6,14},... | collective-permute-start | bytes 393224 | tf_op jit(solution)/shard_map/ppermute | solution.py:640
  13.9 18.4 %collective-permute-start.3 = (bf16[32,2048]{1,0:T(8,128)(2,1)S(1)}, bf16[32,2048]{1,0:T(8,128)(2,1)S(1)}, u32[]{:S(2)}, u32[]{:S(2)}) collective-permute-start(bf16[32,2048]{1,0:T(8,128)(2,1)S(1)} %get-tuple-element.176), channel_id=1, source_target_pairs={{0,4},{4,8},{8,12},{12,0},{1,5},{5,9},{9,13},{13,1},{2,6},{6,10},{... | collective-permute-start | bytes 393224 | tf_op jit(solution)/shard_map/ppermute | solution.py:640
  25.2 11.1 %collective-permute-start.10 = (bf16[128,2048]{1,0:T(8,128)(2,1)S(1)}, bf16[128,2048]{1,0:T(8,128)(2,1)S(1)}, u32[]{:S(2)}, u32[]{:S(2)}) collective-permute-start(bf16[128,2048]{1,0:T(8,128)(2,1)S(1)} %get-tuple-element.95.own), channel_id=1, source_target_pairs={{0,1},{1,0},{2,3},{3,2},{4,5},{5,4},{6,7},{7,6},{8,9},{9,8},{10,11... | collective-permute-start | bytes 1572872 | tf_op jit(solution)/shard_map/ppermute | solution.py:644
  34.7 24.2 %collective-permute-start.7 = (bf16[128,2048]{1,0:T(8,128)(2,1)S(1)}, bf16[128,2048]{1,0:T(8,128)(2,1)S(1)}, u32[]{:S(2)}, u32[]{:S(2)}) collective-permute-start(bf16[128,2048]{1,0:T(8,128)(2,1)S(1)} %maximum_multiply_fusion.dy_own.dy), channel_id=1, source_target_pairs={{0,2},{1,3},{2,0},{3,1},{4,6},{5,7},{6,4},{7,5},{8,10},{9,11},{10,... | collective-permute-start | bytes 1572872 | tf_op jit(solution)/shard_map/ppermute | solution.py:647
  62.5 14.4 %collective-permute-start.14 = (bf16[128,2048]{1,0:T(8,128)(2,1)}, bf16[128,2048]{1,0:T(8,128)(2,1)}, u32[]{:S(2)}, u32[]{:S(2)}) collective-permute-start(bf16[128,2048]{1,0:T(8,128)(2,1)} %shard_map.205), channel_id=1, source_target_pairs={{0,2},{1,3},{2,0},{3,1},{4,6},{5,7},{6,4},{7,5},{8,10},{9,11},{10,... | collective-permute-start | bytes 1572872 | tf_op jit(solution)/shard_map/ppermute | solution.py:647
  64.1 17.2 %collective-permute-start.15 = (bf16[128,2048]{1,0:T(8,128)(2,1)S(1)}, bf16[128,2048]{1,0:T(8,128)(2,1)}, u32[]{:S(2)}, u32[]{:S(2)}) collective-permute-start(bf16[128,2048]{1,0:T(8,128)(2,1)S(1)} %pad_maximum_fusion.1), channel_id=1, source_target_pairs={{0,16},{16,0},{1,17},{17,1},{2,18},{18,2},{3,19},{19,3},{4,20},{20... | collective-permute-start | bytes 1572872 | tf_op jit(solution)/shard_map/ppermute | solution.py:650
  80.7 13.3 %collective-permute-start.17 = (bf16[128,2048]{1,0:T(8,128)(2,1)S(1)}, bf16[128,2048]{1,0:T(8,128)(2,1)}, u32[]{:S(2)}, u32[]{:S(2)}) collective-permute-start(bf16[128,2048]{1,0:T(8,128)(2,1)S(1)} %get-tuple-element.105.own), channel_id=1, source_target_pairs={{0,2},{1,3},{2,0},{3,1},{4,6},{5,7},{6,4},{7,5},{8,10},{9,11},{10,... | collective-permute-start | bytes 1572872 | tf_op jit(solution)/shard_map/ppermute | solution.py:647
  81.2 16.6 %collective-permute-start.16 = (bf16[512,512]{1,0:T(8,128)(2,1)}, bf16[512,512]{1,0:T(8,128)(2,1)}, u32[]{:S(2)}, u32[]{:S(2)}) collective-permute-start(bf16[512,512]{1,0:T(8,128)(2,1)} %get-tuple-element.103), channel_id=1, source_target_pairs={{0,16},{16,0},{1,17},{17,1},{2,18},{18,2},{3,19},{19,3},{4,20},{20... | collective-permute-start | bytes 1572872 | tf_op jit(solution)/shard_map/ppermute | solution.py:650
  82.8 15.1 %collective-permute-start.18 = (bf16[128,2048]{1,0:T(8,128)(2,1)S(1)}, bf16[128,2048]{1,0:T(8,128)(2,1)S(1)}, u32[]{:S(2)}, u32[]{:S(2)}) collective-permute-start(bf16[128,2048]{1,0:T(8,128)(2,1)S(1)} %get-tuple-element.105.own), channel_id=1, source_target_pairs={{0,1},{1,0},{2,3},{3,2},{4,5},{5,4},{6,7},{7,6},{8,9},{9,8},{10,11... | collective-permute-start | bytes 1572872 | tf_op jit(solution)/shard_map/ppermute | solution.py:644
  95.2 37.2 %collective-permute-start.22 = (bf16[128,2048]{1,0:T(8,128)(2,1)}, bf16[128,2048]{1,0:T(8,128)(2,1)S(1)}, u32[]{:S(2)}, u32[]{:S(2)}) collective-permute-start(bf16[128,2048]{1,0:T(8,128)(2,1)} %collective-permute-done.15), channel_id=1, source_target_pairs={{0,1},{1,0},{2,3},{3,2},{4,5},{5,4},{6,7},{7,6},{8,9},{9,8},{10,11... | collective-permute-start | bytes 1572872 | tf_op jit(solution)/shard_map/ppermute | solution.py:644
  95.8 14.1 %collective-permute-start.21 = (bf16[128,2048]{1,0:T(8,128)(2,1)}, bf16[128,2048]{1,0:T(8,128)(2,1)S(1)}, u32[]{:S(2)}, u32[]{:S(2)}) collective-permute-start(bf16[128,2048]{1,0:T(8,128)(2,1)} %collective-permute-done.15), channel_id=1, source_target_pairs={{0,2},{1,3},{2,0},{3,1},{4,6},{5,7},{6,4},{7,5},{8,10},{9,11},{10,... | collective-permute-start | bytes 1572872 | tf_op jit(solution)/shard_map/ppermute | solution.py:647
  106.4 31.0 %collective-permute-start.24 = (bf16[2,512,512]{2,1,0:T(8,128)(2,1)S(1)}, bf16[2,512,512]{2,1,0:T(8,128)(2,1)S(1)}, u32[]{:S(2)}, u32[]{:S(2)}) collective-permute-start(bf16[2,512,512]{2,1,0:T(8,128)(2,1)S(1)} %shard_map.207.refs_6_.refs_2_), channel_id=1, source_target_pairs={{0,16},{16,0},{1,17},{17,1},{2,18},{18,2},{3,19},{19,3},{4,20},{20... | collective-permute-start | bytes 3145736 | tf_op jit(solution)/shard_map/ppermute | solution.py:650
  109.9 24.1 %collective-permute-start.23 = (bf16[128,2048]{1,0:T(8,128)(2,1)S(1)}, bf16[128,2048]{1,0:T(8,128)(2,1)S(1)}, u32[]{:S(2)}, u32[]{:S(2)}) collective-permute-start(bf16[128,2048]{1,0:T(8,128)(2,1)S(1)} %collective-permute-done.21), channel_id=1, source_target_pairs={{0,1},{1,0},{2,3},{3,2},{4,5},{5,4},{6,7},{7,6},{8,9},{9,8},{10,11... | collective-permute-start | bytes 1572872 | tf_op jit(solution)/shard_map/ppermute | solution.py:644
  129.9 28.6 %collective-permute-start.26 = (bf16[128,2048]{1,0:T(8,128)(2,1)S(1)}, bf16[128,2048]{1,0:T(8,128)(2,1)}, u32[]{:S(2)}, u32[]{:S(2)}) collective-permute-start(bf16[128,2048]{1,0:T(8,128)(2,1)S(1)} %get-tuple-element.115), channel_id=1, source_target_pairs={{0,1},{1,0},{2,3},{3,2},{4,5},{5,4},{6,7},{7,6},{8,9},{9,8},{10,11... | collective-permute-start | bytes 1572872 | tf_op jit(solution)/shard_map/ppermute | solution.py:644
  132.4 32.4 %collective-permute-start.28 = (bf16[2,512,512]{2,1,0:T(8,128)(2,1)}, bf16[2,512,512]{2,1,0:T(8,128)(2,1)}, u32[]{:S(2)}, u32[]{:S(2)}) collective-permute-start(bf16[2,512,512]{2,1,0:T(8,128)(2,1)} %slice.111), channel_id=1, source_target_pairs={{0,16},{16,0},{1,17},{17,1},{2,18},{18,2},{3,19},{19,3},{4,20},{20... | collective-permute-start | bytes 3145736 | tf_op jit(solution)/shard_map/ppermute | solution.py:650
  134.9 23.5 %collective-permute-start.27 = (bf16[128,2048]{1,0:T(8,128)(2,1)}, bf16[128,2048]{1,0:T(8,128)(2,1)}, u32[]{:S(2)}, u32[]{:S(2)}) collective-permute-start(bf16[128,2048]{1,0:T(8,128)(2,1)} %shard_map.209), channel_id=1, source_target_pairs={{0,2},{1,3},{2,0},{3,1},{4,6},{5,7},{6,4},{7,5},{8,10},{9,11},{10,... | collective-permute-start | bytes 1572872 | tf_op jit(solution)/shard_map/ppermute | solution.py:647
  141.4 49.2 %collective-permute-start.32 = (bf16[2,768,512]{2,1,0:T(8,128)(2,1)S(1)}, bf16[2,768,512]{2,1,0:T(8,128)(2,1)}, u32[]{:S(2)}, u32[]{:S(2)}) collective-permute-start(bf16[2,768,512]{2,1,0:T(8,128)(2,1)S(1)} %shard_map.210.mine), channel_id=1, source_target_pairs={{0,4},{12,8},{1,5},{13,9},{2,6},{14,10},{3,7},{15,11},{16,20},{28,... | collective-permute-start | bytes 4718600 | tf_op jit(solution)/shard_map/ppermute | solution.py:696
  163.2 13.5 %collective-permute-start.29 = (bf16[128,2048]{1,0:T(8,128)(2,1)S(1)}, bf16[128,2048]{1,0:T(8,128)(2,1)S(1)}, u32[]{:S(2)}, u32[]{:S(2)}) collective-permute-start(bf16[128,2048]{1,0:T(8,128)(2,1)S(1)} %get-tuple-element.124.own), channel_id=1, source_target_pairs={{0,2},{1,3},{2,0},{3,1},{4,6},{5,7},{6,4},{7,5},{8,10},{9,11},{10,... | collective-permute-start | bytes 1572872 | tf_op jit(solution)/shard_map/ppermute | solution.py:647
  164.8 13.3 %collective-permute-start.31 = (bf16[128,2048]{1,0:T(8,128)(2,1)S(1)}, bf16[128,2048]{1,0:T(8,128)(2,1)}, u32[]{:S(2)}, u32[]{:S(2)}) collective-permute-start(bf16[128,2048]{1,0:T(8,128)(2,1)S(1)} %pad_maximum_fusion.2), channel_id=1, source_target_pairs={{0,16},{16,0},{1,17},{17,1},{2,18},{18,2},{3,19},{19,3},{4,20},{20... | collective-permute-start | bytes 1572872 | tf_op jit(solution)/shard_map/ppermute | solution.py:650
  165.4 18.1 %collective-permute-start.25 = (bf16[128,2048]{1,0:T(8,128)(2,1)S(1)}, bf16[128,2048]{1,0:T(8,128)(2,1)S(1)}, u32[]{:S(2)}, u32[]{:S(2)}) collective-permute-start(bf16[128,2048]{1,0:T(8,128)(2,1)S(1)} %get-tuple-element.113), channel_id=1, source_target_pairs={{0,1},{1,0},{2,3},{3,2},{4,5},{5,4},{6,7},{7,6},{8,9},{9,8},{10,11... | collective-permute-start | bytes 1572872 | tf_op jit(solution)/shard_map/ppermute | solution.py:644
  167.0 20.4 %collective-permute-start.33 = (bf16[128,2048]{1,0:T(8,128)(2,1)S(1)}, bf16[128,2048]{1,0:T(8,128)(2,1)S(1)}, u32[]{:S(2)}, u32[]{:S(2)}) collective-permute-start(bf16[128,2048]{1,0:T(8,128)(2,1)S(1)} %get-tuple-element.124.own), channel_id=1, source_target_pairs={{0,1},{1,0},{2,3},{3,2},{4,5},{5,4},{6,7},{7,6},{8,9},{9,8},{10,11... | collective-permute-start | bytes 1572872 | tf_op jit(solution)/shard_map/ppermute | solution.py:644
  178.1 12.5 %collective-permute-start.36 = (bf16[128,2048]{1,0:T(8,128)(2,1)}, bf16[128,2048]{1,0:T(8,128)(2,1)}, u32[]{:S(2)}, u32[]{:S(2)}) collective-permute-start(bf16[128,2048]{1,0:T(8,128)(2,1)} %collective-permute-done.31), channel_id=1, source_target_pairs={{0,2},{1,3},{2,0},{3,1},{4,6},{5,7},{6,4},{7,5},{8,10},{9,11},{10,... | collective-permute-start | bytes 1572872 | tf_op jit(solution)/shard_map/ppermute | solution.py:647
  178.8 13.5 %collective-permute-start.34 = (bf16[128,2048]{1,0:T(8,128)(2,1)S(1)}, bf16[128,2048]{1,0:T(8,128)(2,1)S(1)}, u32[]{:S(2)}, u32[]{:S(2)}) collective-permute-start(bf16[128,2048]{1,0:T(8,128)(2,1)S(1)} %collective-permute-done.29.near), channel_id=1, source_target_pairs={{0,1},{1,0},{2,3},{3,2},{4,5},{5,4},{6,7},{7,6},{8,9},{9,8},{10,11... | collective-permute-start | bytes 1572872 | tf_op jit(solution)/shard_map/ppermute | solution.py:644
  183.5 44.0 %collective-permute-start.45 = (bf16[2,768,512]{2,1,0:T(8,128)(2,1)}, bf16[2,768,512]{2,1,0:T(8,128)(2,1)}, u32[]{:S(2)}, u32[]{:S(2)}) collective-permute-start(bf16[2,768,512]{2,1,0:T(8,128)(2,1)} %shard_map.213.mine), channel_id=1, source_target_pairs={{0,4},{12,8},{1,5},{13,9},{2,6},{14,10},{3,7},{15,11},{16,20},{28,... | collective-permute-start | bytes 4718600 | tf_op jit(solution)/shard_map/ppermute | solution.py:696
  187.4 30.2 %collective-permute-start.39 = (bf16[2,512,512]{2,1,0:T(8,128)(2,1)}, bf16[2,512,512]{2,1,0:T(8,128)(2,1)S(1)}, u32[]{:S(2)}, u32[]{:S(2)}) collective-permute-start(bf16[2,512,512]{2,1,0:T(8,128)(2,1)} %get-tuple-element.132), channel_id=1, source_target_pairs={{0,16},{16,0},{1,17},{17,1},{2,18},{18,2},{3,19},{19,3},{4,20},{20... | collective-permute-start | bytes 3145736 | tf_op jit(solution)/shard_map/ppermute | solution.py:650
  190.6 20.1 %collective-permute-start.37 = (bf16[128,2048]{1,0:T(8,128)(2,1)}, bf16[128,2048]{1,0:T(8,128)(2,1)}, u32[]{:S(2)}, u32[]{:S(2)}) collective-permute-start(bf16[128,2048]{1,0:T(8,128)(2,1)} %collective-permute-done.31), channel_id=1, source_target_pairs={{0,1},{1,0},{2,3},{3,2},{4,5},{5,4},{6,7},{7,6},{8,9},{9,8},{10,11... | collective-permute-start | bytes 1572872 | tf_op jit(solution)/shard_map/ppermute | solution.py:644
  190.6 20.8 %collective-permute-start.38 = (bf16[128,2048]{1,0:T(8,128)(2,1)}, bf16[128,2048]{1,0:T(8,128)(2,1)}, u32[]{:S(2)}, u32[]{:S(2)}) collective-permute-start(bf16[128,2048]{1,0:T(8,128)(2,1)} %collective-permute-done.36), channel_id=1, source_target_pairs={{0,1},{1,0},{2,3},{3,2},{4,5},{5,4},{6,7},{7,6},{8,9},{9,8},{10,11... | collective-permute-start | bytes 1572872 | tf_op jit(solution)/shard_map/ppermute | solution.py:644
  193.0 32.3 %collective-permute-start.40 = (bf16[128,2048]{1,0:T(8,128)(2,1)}, bf16[128,2048]{1,0:T(8,128)(2,1)S(1)}, u32[]{:S(2)}, u32[]{:S(2)}) collective-permute-start(bf16[128,2048]{1,0:T(8,128)(2,1)} %get-tuple-element.136), channel_id=1, source_target_pairs={{0,1},{1,0},{2,3},{3,2},{4,5},{5,4},{6,7},{7,6},{8,9},{9,8},{10,11... | collective-permute-start | bytes 1572872 | tf_op jit(solution)/shard_map/ppermute | solution.py:644
  210.8 14.6 %collective-permute-start.30 = (bf16[128,2048]{1,0:T(8,128)(2,1)}, bf16[128,2048]{1,0:T(8,128)(2,1)S(1)}, u32[]{:S(2)}, u32[]{:S(2)}) collective-permute-start(bf16[128,2048]{1,0:T(8,128)(2,1)} %copy-done.80), channel_id=1, source_target_pairs={{0,2},{1,3},{2,0},{3,1},{4,6},{5,7},{6,4},{7,5},{8,10},{9,11},{10,... | collective-permute-start | bytes 1572872 | tf_op jit(solution)/shard_map/ppermute | solution.py:647
  211.5 10.8 %collective-permute-start.35 = (bf16[128,2048]{1,0:T(8,128)(2,1)}, bf16[128,2048]{1,0:T(8,128)(2,1)S(1)}, u32[]{:S(2)}, u32[]{:S(2)}) collective-permute-start(bf16[128,2048]{1,0:T(8,128)(2,1)} %get-tuple-element.127), channel_id=1, source_target_pairs={{0,1},{1,0},{2,3},{3,2},{4,5},{5,4},{6,7},{7,6},{8,9},{9,8},{10,11... | collective-permute-start | bytes 1572872 | tf_op jit(solution)/shard_map/ppermute | solution.py:644
  217.6 49.4 %collective-permute-start.44 = (bf16[2,512,512]{2,1,0:T(8,128)(2,1)}, bf16[2,512,512]{2,1,0:T(8,128)(2,1)}, u32[]{:S(2)}, u32[]{:S(2)}) collective-permute-start(bf16[2,512,512]{2,1,0:T(8,128)(2,1)} %shard_map.216), channel_id=1, source_target_pairs={{4,8},{8,4},{5,9},{9,5},{6,10},{10,6},{7,11},{11,7},{20,24},{24,20... | collective-permute-start | bytes 3145736 | tf_op jit(solution)/shard_map/ppermute | solution.py:700
  226.3 32.1 %collective-permute-start.46 = (bf16[128,2048]{1,0:T(8,128)(2,1)}, bf16[128,2048]{1,0:T(8,128)(2,1)}, u32[]{:S(2)}, u32[]{:S(2)}) collective-permute-start(bf16[128,2048]{1,0:T(8,128)(2,1)} %get-tuple-element.138), channel_id=1, source_target_pairs={{0,1},{1,0},{2,3},{3,2},{4,5},{5,4},{6,7},{7,6},{8,9},{9,8},{10,11... | collective-permute-start | bytes 1572872 | tf_op jit(solution)/shard_map/ppermute | solution.py:644
  226.3 32.1 %collective-permute-start.47 = (bf16[128,2048]{1,0:T(8,128)(2,1)}, bf16[128,2048]{1,0:T(8,128)(2,1)}, u32[]{:S(2)}, u32[]{:S(2)}) collective-permute-start(bf16[128,2048]{1,0:T(8,128)(2,1)} %shard_map.218), channel_id=1, source_target_pairs={{0,2},{1,3},{2,0},{3,1},{4,6},{5,7},{6,4},{7,5},{8,10},{9,11},{10,... | collective-permute-start | bytes 1572872 | tf_op jit(solution)/shard_map/ppermute | solution.py:647
  227.5 25.0 %collective-permute-start.42 = (bf16[32,2048]{1,0:T(8,128)(2,1)S(1)}, bf16[32,2048]{1,0:T(8,128)(2,1)S(1)}, u32[]{:S(2)}, u32[]{:S(2)}) collective-permute-start(bf16[32,2048]{1,0:T(8,128)(2,1)S(1)} %get-tuple-element.189), channel_id=1, source_target_pairs={{0,8},{4,12},{8,0},{12,4},{1,9},{5,13},{9,1},{13,5},{2,10},{6,14},... | collective-permute-start | bytes 393224 | tf_op jit(solution)/shard_map/ppermute | solution.py:666
  234.4 20.8 %collective-permute-start.41 = (bf16[32,2048]{1,0:T(8,128)(2,1)}, bf16[32,2048]{1,0:T(8,128)(2,1)S(1)}, u32[]{:S(2)}, u32[]{:S(2)}) collective-permute-start(bf16[32,2048]{1,0:T(8,128)(2,1)} %get-tuple-element.190), channel_id=1, source_target_pairs={{0,12},{4,0},{8,4},{12,8},{1,13},{5,1},{9,5},{13,9},{2,14},{6,2},{... | collective-permute-start | bytes 393224 | tf_op jit(solution)/shard_map/ppermute | solution.py:666
  252.6 26.4 %collective-permute-start.49 = (bf16[2,512,512]{2,1,0:T(8,128)(2,1)}, bf16[2,512,512]{2,1,0:T(8,128)(2,1)S(1)}, u32[]{:S(2)}, u32[]{:S(2)}) collective-permute-start(bf16[2,512,512]{2,1,0:T(8,128)(2,1)} %get-tuple-element.144), channel_id=1, source_target_pairs={{0,16},{16,0},{1,17},{17,1},{2,18},{18,2},{3,19},{19,3},{4,20},{20... | collective-permute-start | bytes 3145736 | tf_op jit(solution)/shard_map/ppermute | solution.py:650
  257.0 26.5 %collective-permute-start.50 = (bf16[128,2048]{1,0:T(8,128)(2,1)}, bf16[128,2048]{1,0:T(8,128)(2,1)}, u32[]{:S(2)}, u32[]{:S(2)}) collective-permute-start(bf16[128,2048]{1,0:T(8,128)(2,1)} %pad_maximum_fusion.3.own), channel_id=1, source_target_pairs={{0,2},{1,3},{2,0},{3,1},{4,6},{5,7},{6,4},{7,5},{8,10},{9,11},{10,... | collective-permute-start | bytes 1572872 | tf_op jit(solution)/shard_map/ppermute | solution.py:647
  270.2 54.5 %collective-permute-start.48 = (bf16[2,256,512]{2,1,0:T(8,128)(2,1)}, bf16[2,256,512]{2,1,0:T(8,128)(2,1)}, u32[]{:S(2)}, u32[]{:S(2)}) collective-permute-start(bf16[2,256,512]{2,1,0:T(8,128)(2,1)} %shard_map.222.near), channel_id=1, source_target_pairs={{4,0},{8,12},{5,1},{9,13},{6,2},{10,14},{7,3},{11,15},{20,16},{24,... | collective-permute-start | bytes 1572872 | tf_op jit(solution)/shard_map/ppermute | solution.py:705
  272.9 12.9 %collective-permute-start.55 = (bf16[32,2048]{1,0:T(8,128)(2,1)S(1)}, bf16[32,2048]{1,0:T(8,128)(2,1)S(1)}, u32[]{:S(2)}, u32[]{:S(2)}) collective-permute-start(bf16[32,2048]{1,0:T(8,128)(2,1)S(1)} %get-tuple-element.184), channel_id=1, source_target_pairs={{0,4},{4,8},{8,12},{12,0},{1,5},{5,9},{9,13},{13,1},{2,6},{6,10},{... | collective-permute-start | bytes 393224 | tf_op jit(solution)/shard_map/ppermute | solution.py:666
  278.9 93.8 %collective-permute-start.58 = (bf16[2,768,512]{2,1,0:T(8,128)(2,1)}, bf16[2,768,512]{2,1,0:T(8,128)(2,1)S(1)}, u32[]{:S(2)}, u32[]{:S(2)}) collective-permute-start(bf16[2,768,512]{2,1,0:T(8,128)(2,1)} %copy-done.18), channel_id=1, source_target_pairs={{0,4},{12,8},{1,5},{13,9},{2,6},{14,10},{3,7},{15,11},{16,20},{28,... | collective-permute-start | bytes 4718600 | tf_op jit(solution)/shard_map/ppermute | solution.py:696
  282.8 56.6 %collective-permute-start.56 = (bf16[2,512,512]{2,1,0:T(8,128)(2,1)}, bf16[2,512,512]{2,1,0:T(8,128)(2,1)S(1)}, u32[]{:S(2)}, u32[]{:S(2)}) collective-permute-start(bf16[2,512,512]{2,1,0:T(8,128)(2,1)} %copy-done.72), channel_id=1, source_target_pairs={{4,8},{8,4},{5,9},{9,5},{6,10},{10,6},{7,11},{11,7},{20,24},{24,20... | collective-permute-start | bytes 3145736 | tf_op jit(solution)/shard_map/ppermute | solution.py:700
  283.5 35.9 %collective-permute-start.54 = (bf16[32,2048]{1,0:T(8,128)(2,1)S(1)}, bf16[32,2048]{1,0:T(8,128)(2,1)S(1)}, u32[]{:S(2)}, u32[]{:S(2)}) collective-permute-start(bf16[32,2048]{1,0:T(8,128)(2,1)S(1)} %get-tuple-element.185), channel_id=1, source_target_pairs={{0,8},{4,12},{8,0},{12,4},{1,9},{5,13},{9,1},{13,5},{2,10},{6,14},... | collective-permute-start | bytes 393224 | tf_op jit(solution)/shard_map/ppermute | solution.py:666
  285.8 90.9 %collective-permute-start.62 = (bf16[3,512,512]{2,1,0:T(8,128)(2,1)}, bf16[3,512,512]{2,1,0:T(8,128)(2,1)S(1)}, u32[]{:S(2)}, u32[]{:S(2)}) collective-permute-start(bf16[3,512,512]{2,1,0:T(8,128)(2,1)} %copy-done.14), channel_id=1, source_target_pairs={{0,16},{16,0},{1,17},{17,1},{2,18},{18,2},{3,19},{19,3},{4,20},{20... | collective-permute-start | bytes 4718600 | tf_op jit(solution)/shard_map/ppermute | solution.py:650
  324.6 12.0 %collective-permute-start.52 = (bf16[128,2048]{1,0:T(8,128)(2,1)}, bf16[128,2048]{1,0:T(8,128)(2,1)S(1)}, u32[]{:S(2)}, u32[]{:S(2)}) collective-permute-start(bf16[128,2048]{1,0:T(8,128)(2,1)} %collective-permute-done.50.near), channel_id=1, source_target_pairs={{0,1},{1,0},{2,3},{3,2},{4,5},{5,4},{6,7},{7,6},{8,9},{9,8},{10,11... | collective-permute-start | bytes 1572872 | tf_op jit(solution)/shard_map/ppermute | solution.py:644
  332.1 62.3 %collective-permute-start.67 = (bf16[2,768,512]{2,1,0:T(8,128)(2,1)S(1)}, bf16[2,768,512]{2,1,0:T(8,128)(2,1)S(1)}, u32[]{:S(2)}, u32[]{:S(2)}) collective-permute-start(bf16[2,768,512]{2,1,0:T(8,128)(2,1)S(1)} %shard_map.223.mine), channel_id=1, source_target_pairs={{0,4},{12,8},{1,5},{13,9},{2,6},{14,10},{3,7},{15,11},{16,20},{28,... | collective-permute-start | bytes 4718600 | tf_op jit(solution)/shard_map/ppermute | solution.py:696
  336.6 34.8 %collective-permute-start.61 = (f32[15360]{0:T(1024)S(1)}, f32[15360]{0:T(1024)S(1)}, u32[]{:S(2)}, u32[]{:S(2)}) collective-permute-start(f32[15360]{0:T(1024)S(1)} %pad_maximum_fusion.6), channel_id=1, source_target_pairs={{0,4},{4,0},{8,12},{12,8},{1,5},{5,1},{9,13},{13,9},{2,6},{6,2},{1... | collective-permute-start | bytes 184328 | tf_op jit(solution)/shard_map/ppermute | solution.py:823
  339.4 43.0 %collective-permute-start.63 = (bf16[128,2048]{1,0:T(8,128)(2,1)S(1)}, bf16[128,2048]{1,0:T(8,128)(2,1)S(1)}, u32[]{:S(2)}, u32[]{:S(2)}) collective-permute-start(bf16[128,2048]{1,0:T(8,128)(2,1)S(1)} %pad_maximum_fusion.4.own), channel_id=1, source_target_pairs={{0,2},{1,3},{2,0},{3,1},{4,6},{5,7},{6,4},{7,5},{8,10},{9,11},{10,... | collective-permute-start | bytes 1572872 | tf_op jit(solution)/shard_map/ppermute | solution.py:647
  371.4 16.3 %collective-permute-start.57 = (bf16[2,256,512]{2,1,0:T(8,128)(2,1)S(1)}, bf16[2,256,512]{2,1,0:T(8,128)(2,1)S(1)}, u32[]{:S(2)}, u32[]{:S(2)}) collective-permute-start(bf16[2,256,512]{2,1,0:T(8,128)(2,1)S(1)} %shard_map.226.near), channel_id=1, source_target_pairs={{4,0},{8,12},{5,1},{9,13},{6,2},{10,14},{7,3},{11,15},{20,16},{24,... | collective-permute-start | bytes 1572872 | tf_op jit(solution)/shard_map/ppermute | solution.py:705
  379.5 41.1 %collective-permute-start.70 = (bf16[2,768,512]{2,1,0:T(8,128)(2,1)S(1)}, bf16[2,768,512]{2,1,0:T(8,128)(2,1)S(1)}, u32[]{:S(2)}, u32[]{:S(2)}) collective-permute-start(bf16[2,768,512]{2,1,0:T(8,128)(2,1)S(1)} %shard_map.227.mine), channel_id=1, source_target_pairs={{0,4},{12,8},{1,5},{13,9},{2,6},{14,10},{3,7},{15,11},{16,20},{28,... | collective-permute-start | bytes 4718600 | tf_op jit(solution)/shard_map/ppermute | solution.py:696
  381.4 17.2 %collective-permute-start.72 = (bf16[2,512,512]{2,1,0:T(8,128)(2,1)S(1)}, bf16[2,512,512]{2,1,0:T(8,128)(2,1)S(1)}, u32[]{:S(2)}, u32[]{:S(2)}) collective-permute-start(bf16[2,512,512]{2,1,0:T(8,128)(2,1)S(1)} %shard_map.228), channel_id=1, source_target_pairs={{4,8},{8,4},{5,9},{9,5},{6,10},{10,6},{7,11},{11,7},{20,24},{24,20... | collective-permute-start | bytes 3145736 | tf_op jit(solution)/shard_map/ppermute | solution.py:700
  397.7 29.3 %collective-permute-start.69 = (bf16[2,512,512]{2,1,0:T(8,128)(2,1)S(1)}, bf16[2,512,512]{2,1,0:T(8,128)(2,1)S(1)}, u32[]{:S(2)}, u32[]{:S(2)}) collective-permute-start(bf16[2,512,512]{2,1,0:T(8,128)(2,1)S(1)} %shard_map.233), channel_id=1, source_target_pairs={{4,8},{8,4},{5,9},{9,5},{6,10},{10,6},{7,11},{11,7},{20,24},{24,20... | collective-permute-start | bytes 3145736 | tf_op jit(solution)/shard_map/ppermute | solution.py:700
  401.1 18.5 %collective-permute-start.73 = (bf16[2,256,512]{2,1,0:T(8,128)(2,1)S(1)}, bf16[2,256,512]{2,1,0:T(8,128)(2,1)S(1)}, u32[]{:S(2)}, u32[]{:S(2)}) collective-permute-start(bf16[2,256,512]{2,1,0:T(8,128)(2,1)S(1)} %shard_map.234.near), channel_id=1, source_target_pairs={{4,0},{8,12},{5,1},{9,13},{6,2},{10,14},{7,3},{11,15},{20,16},{24,... | collective-permute-start | bytes 1572872 | tf_op jit(solution)/shard_map/ppermute | solution.py:705
  420.9 23.5 %collective-permute-start.77 = (bf16[2,512,512]{2,1,0:T(8,128)(2,1)S(1)}, bf16[2,512,512]{2,1,0:T(8,128)(2,1)S(1)}, u32[]{:S(2)}, u32[]{:S(2)}) collective-permute-start(bf16[2,512,512]{2,1,0:T(8,128)(2,1)S(1)} %shard_map.236), channel_id=1, source_target_pairs={{4,8},{8,4},{5,9},{9,5},{6,10},{10,6},{7,11},{11,7},{20,24},{24,20... | collective-permute-start | bytes 3145736 | tf_op jit(solution)/shard_map/ppermute | solution.py:700
  421.6 21.9 %collective-permute-start.66 = (bf16[1,768,512]{2,1,0:T(8,128)(2,1)S(1)}, bf16[1,768,512]{2,1,0:T(8,128)(2,1)S(1)}, u32[]{:S(2)}, u32[]{:S(2)}) collective-permute-start(bf16[1,768,512]{2,1,0:T(8,128)(2,1)S(1)} %shard_map.231.mine), channel_id=1, source_target_pairs={{0,4},{12,8},{1,5},{13,9},{2,6},{14,10},{3,7},{15,11},{16,20},{28,... | collective-permute-start | bytes 2359304 | tf_op jit(solution)/shard_map/ppermute | solution.py:696
  425.6 28.4 %collective-permute-start.76 = (bf16[1,768,512]{2,1,0:T(8,128)(2,1)S(1)}, bf16[1,768,512]{2,1,0:T(8,128)(2,1)S(1)}, u32[]{:S(2)}, u32[]{:S(2)}) collective-permute-start(bf16[1,768,512]{2,1,0:T(8,128)(2,1)S(1)} %shard_map.232.mine), channel_id=1, source_target_pairs={{0,4},{12,8},{1,5},{13,9},{2,6},{14,10},{3,7},{15,11},{16,20},{28,... | collective-permute-start | bytes 2359304 | tf_op jit(solution)/shard_map/ppermute | solution.py:696
  428.6 13.4 %collective-permute-start.74 = (bf16[2,256,512]{2,1,0:T(8,128)(2,1)S(1)}, bf16[2,256,512]{2,1,0:T(8,128)(2,1)S(1)}, u32[]{:S(2)}, u32[]{:S(2)}) collective-permute-start(bf16[2,256,512]{2,1,0:T(8,128)(2,1)S(1)} %shard_map.237.near), channel_id=1, source_target_pairs={{4,0},{8,12},{5,1},{9,13},{6,2},{10,14},{7,3},{11,15},{20,16},{24,... | collective-permute-start | bytes 1572872 | tf_op jit(solution)/shard_map/ppermute | solution.py:705
  443.7 12.5 %collective-permute-start.75 = (bf16[1,512,512]{2,1,0:T(8,128)(2,1)S(1)}, bf16[1,512,512]{2,1,0:T(8,128)(2,1)S(1)}, u32[]{:S(2)}, u32[]{:S(2)}) collective-permute-start(bf16[1,512,512]{2,1,0:T(8,128)(2,1)S(1)} %shard_map.239), channel_id=1, source_target_pairs={{4,8},{8,4},{5,9},{9,5},{6,10},{10,6},{7,11},{11,7},{20,24},{24,20... | collective-permute-start | bytes 1572872 | tf_op jit(solution)/shard_map/ppermute | solution.py:700
  446.0 18.5 %collective-permute-start.80 = (bf16[2,256,512]{2,1,0:T(8,128)(2,1)S(1)}, bf16[2,256,512]{2,1,0:T(8,128)(2,1)S(1)}, u32[]{:S(2)}, u32[]{:S(2)}) collective-permute-start(bf16[2,256,512]{2,1,0:T(8,128)(2,1)S(1)} %shard_map.240.near), channel_id=1, source_target_pairs={{4,0},{8,12},{5,1},{9,13},{6,2},{10,14},{7,3},{11,15},{20,16},{24,... | collective-permute-start | bytes 1572872 | tf_op jit(solution)/shard_map/ppermute | solution.py:705
  457.9 14.7 %collective-permute-start.78 = (bf16[1,256,512]{2,1,0:T(8,128)(2,1)}, bf16[1,256,512]{2,1,0:T(8,128)(2,1)}, u32[]{:S(2)}, u32[]{:S(2)}) collective-permute-start(bf16[1,256,512]{2,1,0:T(8,128)(2,1)} %shard_map.242.near), channel_id=1, source_target_pairs={{4,0},{8,12},{5,1},{9,13},{6,2},{10,14},{7,3},{11,15},{20,16},{24,... | collective-permute-start | bytes 786440 | tf_op jit(solution)/shard_map/ppermute | solution.py:705
  468.5 14.5 %collective-permute-start.81 = (bf16[1,256,512]{2,1,0:T(8,128)(2,1)}, bf16[1,256,512]{2,1,0:T(8,128)(2,1)}, u32[]{:S(2)}, u32[]{:S(2)}) collective-permute-start(bf16[1,256,512]{2,1,0:T(8,128)(2,1)} %shard_map.244.near), channel_id=1, source_target_pairs={{4,0},{8,12},{5,1},{9,13},{6,2},{10,14},{7,3},{11,15},{20,16},{24,... | collective-permute-start | bytes 786440 | tf_op jit(solution)/shard_map/ppermute | solution.py:705
  (111 other events, 1143.9 us)
